TPU v7x, 256 devices: a whole 4x4x8 slice. The times are simulated.
256 devices in a mesh: band: 16 (over z, y_lo), gblk: 16 (over x, y_hi, core).
Axes of the slice: x: 4, y: 4 (y_hi: 2, y_lo: 2; y = y_hi * 2 + y_lo), z: 8, core: 2. Of those that a mesh axis runs over, the one named last changes fastest.
Arguments:
- psi_val: bfloat16 [128, 1024], P('band'), may hold values from -6 to 6
- psi_con: bfloat16 [64, 1024], P('band'), may hold values from -6 to 6
- val_energy: float32 [128], P('band'), may hold values from -12 to -1
- con_energy: float32 [64], P('band'), may hold values from 1 to 30
- sphere_basis: bfloat16 [1024, 61440], P(None, 'gblk'), may hold values from -0.1875 to 0.1875
- block_owner: int32 [480], replicated, may hold values from 0 to 15, as said below
- block_fill: int32 [480], replicated, may hold values from 32 to 128
Outputs:
- polarizability: float32 [98304, 256], P('gblk', 'band')
Inputs may be any that keep to these rules, and one draw needn't show every extreme that they name: `block_owner`: producer p holds blocks p * 480 / 16 onward; it gives at most 3 of them to any owner, and one owner receives exactly 3 from every producer.
All inputs are finite; a program needn't handle non-finite values.
Results may differ from a plain program's by a relative error of at most 0.008.
Values may be sent and summed in bfloat16 or wider, within the bound.
A program may use at most 128 MiB of HBM per device.

v0:
```python
import math

import jax
import jax.numpy as jnp
from jax import lax
from jax.sharding import PartitionSpec as P

W = 256
BLK = 128


def spread(block, axis, holder):
    block = jnp.where(lax.axis_index(axis) == holder, block, jnp.zeros_like(block))
    return lax.psum(block, axis)


def from_behind(value, axis, steps):
    count = lax.axis_size(axis)
    pairs = [(source, (source + steps) % count) for source in range(count)]
    return lax.ppermute(value, axis, pairs)


def block_ranks(owner_table):
    block_cols = owner_table.shape[1]
    same_owner = owner_table[:, :, None] == owner_table[:, None, :]
    earlier = jnp.arange(block_cols)[None, :] < jnp.arange(block_cols)[:, None]
    return jnp.sum((same_owner & earlier[None]).astype(jnp.int32), axis=2)


def band_reduce(partial_rows):
    return lax.psum_scatter(partial_rows, "band", scatter_dimension=1, tiled=True)


def per_device(psi_val, psi_con, val_energy, con_energy, sphere_basis, block_owner, block_fill):
    band_count = lax.axis_size("band")
    gblk_count = lax.axis_size("gblk")
    gblk_rank = lax.axis_index("gblk")
    val_count, grid_points = psi_val.shape
    con_count = psi_con.shape[0]
    local_cols = sphere_basis.shape[1]
    blocks_local = local_cols // BLK
    block_total = block_owner.shape[0]
    capacity = max(2, 2 * block_total // (gblk_count * gblk_count))
    factor = 1.0 / math.sqrt(val_count * band_count * con_count * band_count)
    pair_count = val_count * con_count
    slot_rows = gblk_count * capacity * BLK
    live_all = (jnp.arange(BLK)[None, :] < block_fill[:, None]).astype(jnp.float32)
    my_live = lax.dynamic_slice_in_dim(live_all, gblk_rank * blocks_local, blocks_local, 0).reshape(
        local_cols
    )
    window_live = live_all[: W // BLK].reshape(W)
    window_table = spread(sphere_basis[:, :W], "gblk", 0)
    owner_table = block_owner.reshape(gblk_count, blocks_local)
    rank_table = block_ranks(owner_table)
    dest_ids = jnp.arange(gblk_count)
    slot_ids = jnp.arange(capacity)
    owners_mine = lax.dynamic_slice_in_dim(owner_table, gblk_rank, 1, 0)[0]
    ranks_mine = lax.dynamic_slice_in_dim(rank_table, gblk_rank, 1, 0)[0]
    send_select = (
        (owners_mine[None, None, :] == dest_ids[:, None, None])
        & (ranks_mine[None, None, :] == slot_ids[None, :, None])
    ).astype(jnp.float32)
    conduction = psi_con.astype(jnp.float32)

    def project_band(val_rows, val_energies):
        pair_rows = (
            (val_rows.astype(jnp.float32)[:, None, :] * conduction[None, :, :])
            .astype(jnp.bfloat16)
            .reshape(pair_count, grid_points)
        )
        window_dens = (
            jnp.dot(pair_rows, window_table, preferred_element_type=jnp.float32) * window_live
        ).astype(jnp.bfloat16)
        weight = (factor / (val_energies[:, None] - con_energy[None, :])).reshape(pair_count, 1)
        scaled = (weight * window_dens.astype(jnp.float32)).astype(jnp.bfloat16)
        densities = (
            jnp.dot(pair_rows, sphere_basis, preferred_element_type=jnp.float32) * my_live
        ).astype(jnp.bfloat16)
        outgoing = jnp.einsum(
            "pjb,osj->posb",
            densities.reshape(pair_count, blocks_local, BLK),
            send_select.astype(jnp.bfloat16),
            preferred_element_type=jnp.float32,
        )
        outgoing = outgoing.astype(jnp.bfloat16).reshape(pair_count, gblk_count, capacity * BLK)
        produced = lax.all_to_all(
            outgoing, "gblk", split_axis=1, concat_axis=1, tiled=True
        ).reshape(pair_count, slot_rows)
        return (produced, scaled)

    def record_band(turn_index, val_rows, val_energies, produced_all, scaled_all):
        produced, scaled = project_band(val_rows, val_energies)
        produced_all = lax.dynamic_update_slice_in_dim(
            produced_all, produced, turn_index * pair_count, 0
        )
        scaled_all = lax.dynamic_update_slice_in_dim(scaled_all, scaled, turn_index * pair_count, 0)
        return (produced_all, scaled_all)

    produced_start = jnp.zeros((band_count * pair_count, slot_rows), jnp.bfloat16)
    scaled_start = jnp.zeros((band_count * pair_count, W), jnp.bfloat16)

    def cycle_turn(turn_index, state_tuple):
        val_rows, val_energies, produced_all, scaled_all = state_tuple
        produced_all, scaled_all = record_band(
            turn_index, val_rows, val_energies, produced_all, scaled_all
        )
        val_rows, val_energies = (
            from_behind(val_rows, "band", 1),
            from_behind(val_energies.astype(jnp.bfloat16), "band", 1).astype(val_energies.dtype),
        )
        return (val_rows, val_energies, produced_all, scaled_all)

    val_rows, val_energies, produced_all, scaled_all = lax.fori_loop(
        0, band_count - 1, cycle_turn, (psi_val, val_energy, produced_start, scaled_start)
    )
    produced_all, scaled_all = record_band(
        band_count - 1, val_rows, val_energies, produced_all, scaled_all
    )
    partial_rows = lax.dot_general(
        produced_all, scaled_all, (((0,), (0,)), ((), ())), preferred_element_type=jnp.float32
    )
    return band_reduce(partial_rows)


def solution(mesh):
    return jax.shard_map(
        per_device,
        mesh=mesh,
        in_specs=(
            P("band", None),
            P("band", None),
            P("band"),
            P("band"),
            P(None, "gblk"),
            P(),
            P(),
        ),
        out_specs=P("gblk", "band"),
        check_vma=False,
    )
```

profile of v0, /device:TPU:1, one launch (start us, length us, event | category | flops | bytes accessed | tf_op | source)
XLA Modules:
  0.0 700.0 jit_solution(13650656624937714341)
XLA Ops:
  11.8 145.5 %all-reduce.2.cloned.1.call-done = bf16[1024,256]{1,0:T(8,128)(2,1)} async-done(((bf16[1024,256]{1,0:T(8,128)(2,1)}), bf16[1024,256]{1,0:T(8,128)(2,1)}) %all-reduce.2.cloned.1.call-update) | async-done | bytes 524304 | tf_op jit(solution)/shard_map/psum | solution.py:14
  160.8 367.5 %while.22 = (s32[]{:T(128)}, bf16[8,1024]{1,0:T(8,128)(2,1)S(1)}, f32[8]{0:T(128)S(1)}, bf16[512,6144]{1,0:T(8,128)(2,1)}, bf16[512,256]{1,0:T(8,128)(2,1)S(1)},...) while((s32[]{:T(128)}, bf16[8,1024]{1,0:T(8,128)(2,1)S(1)}, ...), condition=%wide.region_3.4_spmd.clone, body=%wide.region_2.3_spmd.clone.sunk | while | flops 280793408 | bytes 14649293 | solution.py:113
  169.9 7.2 %all-to-all-start = ((bf16[32,16,384]{2,0,1:T(8,128)(2,1)}), bf16[32,16,384]{2,0,1:T(8,128)(2,1)S(1)}, u32[]{:S(2)}, u32[]{:S(2)}) async-start(bf16[32,16,384]{2,0,1:T(8,128)(2,1)} %reshape.201), calls=%async_computation | async-start | bytes 786432 | tf_op jit(solution)/shard_map/while/body/eval_jaxpr/all_to_all | solution.py:86
  177.5 9.7 %all-to-all-done = bf16[32,16,384]{2,0,1:T(8,128)(2,1)S(1)} async-done(((bf16[32,16,384]{2,0,1:T(8,128)(2,1)}), bf16[32,16,384]{2,0,1:T(8,128)(2,1)S(1)}, u32[]{:S(2)}, u32[]{:S(2)}) %all-to-all-start) | async-done | bytes 393248 | tf_op jit(solution)/shard_map/while/body/eval_jaxpr/all_to_all | solution.py:86
  202.0 9.7 %all-to-all-done = bf16[32,16,384]{2,0,1:T(8,128)(2,1)S(1)} async-done(((bf16[32,16,384]{2,0,1:T(8,128)(2,1)}), bf16[32,16,384]{2,0,1:T(8,128)(2,1)S(1)}, u32[]{:S(2)}, u32[]{:S(2)}) %all-to-all-start) | async-done | bytes 393248 | tf_op jit(solution)/shard_map/while/body/eval_jaxpr/all_to_all | solution.py:86
  221.6 4.7 all-to-all-start
  226.7 9.7 %all-to-all-done = bf16[32,16,384]{2,0,1:T(8,128)(2,1)S(1)} async-done(((bf16[32,16,384]{2,0,1:T(8,128)(2,1)}), bf16[32,16,384]{2,0,1:T(8,128)(2,1)S(1)}, u32[]{:S(2)}, u32[]{:S(2)}) %all-to-all-start) | async-done | bytes 393248 | tf_op jit(solution)/shard_map/while/body/eval_jaxpr/all_to_all | solution.py:86
  247.5 4.7 all-to-all-start
  252.5 9.7 %all-to-all-done = bf16[32,16,384]{2,0,1:T(8,128)(2,1)S(1)} async-done(((bf16[32,16,384]{2,0,1:T(8,128)(2,1)}), bf16[32,16,384]{2,0,1:T(8,128)(2,1)S(1)}, u32[]{:S(2)}, u32[]{:S(2)}) %all-to-all-start) | async-done | bytes 393248 | tf_op jit(solution)/shard_map/while/body/eval_jaxpr/all_to_all | solution.py:86
  271.2 4.7 all-to-all-start
  276.3 9.7 %all-to-all-done = bf16[32,16,384]{2,0,1:T(8,128)(2,1)S(1)} async-done(((bf16[32,16,384]{2,0,1:T(8,128)(2,1)}), bf16[32,16,384]{2,0,1:T(8,128)(2,1)S(1)}, u32[]{:S(2)}, u32[]{:S(2)}) %all-to-all-start) | async-done | bytes 393248 | tf_op jit(solution)/shard_map/while/body/eval_jaxpr/all_to_all | solution.py:86
  294.9 4.7 all-to-all-start
  300.0 9.8 %all-to-all-done = bf16[32,16,384]{2,0,1:T(8,128)(2,1)S(1)} async-done(((bf16[32,16,384]{2,0,1:T(8,128)(2,1)}), bf16[32,16,384]{2,0,1:T(8,128)(2,1)S(1)}, u32[]{:S(2)}, u32[]{:S(2)}) %all-to-all-start) | async-done | bytes 393248 | tf_op jit(solution)/shard_map/while/body/eval_jaxpr/all_to_all | solution.py:86
  318.7 4.7 all-to-all-start
  323.8 9.8 %all-to-all-done = bf16[32,16,384]{2,0,1:T(8,128)(2,1)S(1)} async-done(((bf16[32,16,384]{2,0,1:T(8,128)(2,1)}), bf16[32,16,384]{2,0,1:T(8,128)(2,1)S(1)}, u32[]{:S(2)}, u32[]{:S(2)}) %all-to-all-start) | async-done | bytes 393248 | tf_op jit(solution)/shard_map/while/body/eval_jaxpr/all_to_all | solution.py:86
  346.9 9.7 %all-to-all-done = bf16[32,16,384]{2,0,1:T(8,128)(2,1)S(1)} async-done(((bf16[32,16,384]{2,0,1:T(8,128)(2,1)}), bf16[32,16,384]{2,0,1:T(8,128)(2,1)S(1)}, u32[]{:S(2)}, u32[]{:S(2)}) %all-to-all-start) | async-done | bytes 393248 | tf_op jit(solution)/shard_map/while/body/eval_jaxpr/all_to_all | solution.py:86
  366.3 4.7 all-to-all-start
  371.4 9.8 %all-to-all-done = bf16[32,16,384]{2,0,1:T(8,128)(2,1)S(1)} async-done(((bf16[32,16,384]{2,0,1:T(8,128)(2,1)}), bf16[32,16,384]{2,0,1:T(8,128)(2,1)S(1)}, u32[]{:S(2)}, u32[]{:S(2)}) %all-to-all-start) | async-done | bytes 393248 | tf_op jit(solution)/shard_map/while/body/eval_jaxpr/all_to_all | solution.py:86
  391.0 4.7 all-to-all-start
  396.0 9.7 %all-to-all-done = bf16[32,16,384]{2,0,1:T(8,128)(2,1)S(1)} async-done(((bf16[32,16,384]{2,0,1:T(8,128)(2,1)}), bf16[32,16,384]{2,0,1:T(8,128)(2,1)S(1)}, u32[]{:S(2)}, u32[]{:S(2)}) %all-to-all-start) | async-done | bytes 393248 | tf_op jit(solution)/shard_map/while/body/eval_jaxpr/all_to_all | solution.py:86
  415.6 4.7 all-to-all-start
  420.7 9.8 %all-to-all-done = bf16[32,16,384]{2,0,1:T(8,128)(2,1)S(1)} async-done(((bf16[32,16,384]{2,0,1:T(8,128)(2,1)}), bf16[32,16,384]{2,0,1:T(8,128)(2,1)S(1)}, u32[]{:S(2)}, u32[]{:S(2)}) %all-to-all-start) | async-done | bytes 393248 | tf_op jit(solution)/shard_map/while/body/eval_jaxpr/all_to_all | solution.py:86
  441.4 4.7 all-to-all-start
  446.5 9.8 %all-to-all-done = bf16[32,16,384]{2,0,1:T(8,128)(2,1)S(1)} async-done(((bf16[32,16,384]{2,0,1:T(8,128)(2,1)}), bf16[32,16,384]{2,0,1:T(8,128)(2,1)S(1)}, u32[]{:S(2)}, u32[]{:S(2)}) %all-to-all-start) | async-done | bytes 393248 | tf_op jit(solution)/shard_map/while/body/eval_jaxpr/all_to_all | solution.py:86
  465.2 4.7 all-to-all-start
  470.2 9.7 %all-to-all-done = bf16[32,16,384]{2,0,1:T(8,128)(2,1)S(1)} async-done(((bf16[32,16,384]{2,0,1:T(8,128)(2,1)}), bf16[32,16,384]{2,0,1:T(8,128)(2,1)S(1)}, u32[]{:S(2)}, u32[]{:S(2)}) %all-to-all-start) | async-done | bytes 393248 | tf_op jit(solution)/shard_map/while/body/eval_jaxpr/all_to_all | solution.py:86
  494.0 9.7 %all-to-all-done = bf16[32,16,384]{2,0,1:T(8,128)(2,1)S(1)} async-done(((bf16[32,16,384]{2,0,1:T(8,128)(2,1)}), bf16[32,16,384]{2,0,1:T(8,128)(2,1)S(1)}, u32[]{:S(2)}, u32[]{:S(2)}) %all-to-all-start) | async-done | bytes 393248 | tf_op jit(solution)/shard_map/while/body/eval_jaxpr/all_to_all | solution.py:86
  512.7 4.7 all-to-all-start
  517.7 9.7 %all-to-all-done = bf16[32,16,384]{2,0,1:T(8,128)(2,1)S(1)} async-done(((bf16[32,16,384]{2,0,1:T(8,128)(2,1)}), bf16[32,16,384]{2,0,1:T(8,128)(2,1)S(1)}, u32[]{:S(2)}, u32[]{:S(2)}) %all-to-all-start) | async-done | bytes 393248 | tf_op jit(solution)/shard_map/while/body/eval_jaxpr/all_to_all | solution.py:86
  539.5 9.7 %all-to-all-done.1 = bf16[32,16,384]{2,0,1:T(8,128)(2,1)S(1)} async-done(((bf16[32,16,384]{2,0,1:T(8,128)(2,1)}), bf16[32,16,384]{2,0,1:T(8,128)(2,1)S(1)}, u32[]{:S(2)}, u32[]{:S(2)}) %all-to-all-start.1) | async-done | bytes 393248 | tf_op jit(solution)/shard_map/all_to_all | solution.py:86
  550.0 7.3 %fusion.27 = f32[6144,256]{0,1:T(8,128)} fusion(bf16[512,6144]{1,0:T(8,128)(2,1)} %constant_dynamic-update-slice_fusion.1, bf16[512,256]{1,0:T(8,128)(2,1)S(1)} %fusion.20), kind=kOutput, calls=%fused_computation.48 | convolution fusion | flops 1610612736 | bytes 12845056 | tf_op jit(solution)/shard_map/dot_general | solution.py:119
  557.3 135.8 %reduce-scatter.2.cloned.1.call-done = f32[6144,16]{0,1:T(8,128)} async-done(((f32[6144,256]{0,1:T(8,128)}), f32[6144,16]{0,1:T(8,128)}) %reduce-scatter.2.cloned.1.call-update) | async-done | bytes 393232 | tf_op jit(solution)/shard_map/reduce_scatter | solution.py:31
  (345 shorter events, 182.0 us)
Async XLA Ops:
  6.5 150.8 %all-reduce.2.cloned.1.call-start = ((), (), s32[]{:S(2)}) async-start(), calls=%async_computation.3 | async-start | bytes 1048576 | tf_op jit(solution)/shard_map/psum | solution.py:14
  160.8 16.7 %collective-permute-start.1 = (bf16[8]{0:T(256)(128)(2,1)S(1)}, bf16[8]{0:T(256)(128)(2,1)S(1)}, u32[]{:S(2)}, u32[]{:S(2)}) collective-permute-start(bf16[8]{0:T(256)(128)(2,1)S(1)} %convert_element_type.257), channel_id=1, source_target_pairs={{0,16},{16,32},{32,48},{48,64},{64,80},{80,96},{96,112},{112,128},... | collective-permute-start | bytes 56 | tf_op jit(solution)/shard_map/while/body/eval_jaxpr/ppermute | solution.py:20
  161.2 26.8 %collective-permute-start = (bf16[8,1024]{1,0:T(8,128)(2,1)S(1)}, bf16[8,1024]{1,0:T(8,128)(2,1)S(1)}, u32[]{:S(2)}, u32[]{:S(2)}) collective-permute-start(bf16[8,1024]{1,0:T(8,128)(2,1)S(1)} %copy.55), channel_id=1, source_target_pairs={{0,16},{16,32},{32,48},{48,64},{64,80},{80,96},{96,112},{112,128},... | collective-permute-start | bytes 49160 | tf_op jit(solution)/shard_map/while/body/eval_jaxpr/ppermute | solution.py:20
  169.9 17.3 %all-to-all-start = ((bf16[32,16,384]{2,0,1:T(8,128)(2,1)}), bf16[32,16,384]{2,0,1:T(8,128)(2,1)S(1)}, u32[]{:S(2)}, u32[]{:S(2)}) async-start(bf16[32,16,384]{2,0,1:T(8,128)(2,1)} %reshape.201), calls=%async_computation | async-start | bytes 786432 | tf_op jit(solution)/shard_map/while/body/eval_jaxpr/all_to_all | solution.py:86
  188.4 24.3 %collective-permute-start = (bf16[8,1024]{1,0:T(8,128)(2,1)S(1)}, bf16[8,1024]{1,0:T(8,128)(2,1)S(1)}, u32[]{:S(2)}, u32[]{:S(2)}) collective-permute-start(bf16[8,1024]{1,0:T(8,128)(2,1)S(1)} %copy.55), channel_id=1, source_target_pairs={{0,16},{16,32},{32,48},{48,64},{64,80},{80,96},{96,112},{112,128},... | collective-permute-start | bytes 49160 | tf_op jit(solution)/shard_map/while/body/eval_jaxpr/ppermute | solution.py:20
  212.9 24.3 %collective-permute-start = (bf16[8,1024]{1,0:T(8,128)(2,1)S(1)}, bf16[8,1024]{1,0:T(8,128)(2,1)S(1)}, u32[]{:S(2)}, u32[]{:S(2)}) collective-permute-start(bf16[8,1024]{1,0:T(8,128)(2,1)S(1)} %copy.55), channel_id=1, source_target_pairs={{0,16},{16,32},{32,48},{48,64},{64,80},{80,96},{96,112},{112,128},... | collective-permute-start | bytes 49160 | tf_op jit(solution)/shard_map/while/body/eval_jaxpr/ppermute | solution.py:20
  221.6 14.8 %all-to-all-start = ((bf16[32,16,384]{2,0,1:T(8,128)(2,1)}), bf16[32,16,384]{2,0,1:T(8,128)(2,1)S(1)}, u32[]{:S(2)}, u32[]{:S(2)}) async-start(bf16[32,16,384]{2,0,1:T(8,128)(2,1)} %reshape.201), calls=%async_computation | async-start | bytes 786432 | tf_op jit(solution)/shard_map/while/body/eval_jaxpr/all_to_all | solution.py:86
  237.3 15.2 %collective-permute-start.1 = (bf16[8]{0:T(256)(128)(2,1)S(1)}, bf16[8]{0:T(256)(128)(2,1)S(1)}, u32[]{:S(2)}, u32[]{:S(2)}) collective-permute-start(bf16[8]{0:T(256)(128)(2,1)S(1)} %convert_element_type.257), channel_id=1, source_target_pairs={{0,16},{16,32},{32,48},{48,64},{64,80},{80,96},{96,112},{112,128},... | collective-permute-start | bytes 56 | tf_op jit(solution)/shard_map/while/body/eval_jaxpr/ppermute | solution.py:20
  237.6 25.5 %collective-permute-start = (bf16[8,1024]{1,0:T(8,128)(2,1)S(1)}, bf16[8,1024]{1,0:T(8,128)(2,1)S(1)}, u32[]{:S(2)}, u32[]{:S(2)}) collective-permute-start(bf16[8,1024]{1,0:T(8,128)(2,1)S(1)} %copy.55), channel_id=1, source_target_pairs={{0,16},{16,32},{32,48},{48,64},{64,80},{80,96},{96,112},{112,128},... | collective-permute-start | bytes 49160 | tf_op jit(solution)/shard_map/while/body/eval_jaxpr/ppermute | solution.py:20
  247.5 14.8 %all-to-all-start = ((bf16[32,16,384]{2,0,1:T(8,128)(2,1)}), bf16[32,16,384]{2,0,1:T(8,128)(2,1)S(1)}, u32[]{:S(2)}, u32[]{:S(2)}) async-start(bf16[32,16,384]{2,0,1:T(8,128)(2,1)} %reshape.201), calls=%async_computation | async-start | bytes 786432 | tf_op jit(solution)/shard_map/while/body/eval_jaxpr/all_to_all | solution.py:86
  263.4 23.4 %collective-permute-start = (bf16[8,1024]{1,0:T(8,128)(2,1)S(1)}, bf16[8,1024]{1,0:T(8,128)(2,1)S(1)}, u32[]{:S(2)}, u32[]{:S(2)}) collective-permute-start(bf16[8,1024]{1,0:T(8,128)(2,1)S(1)} %copy.55), channel_id=1, source_target_pairs={{0,16},{16,32},{32,48},{48,64},{64,80},{80,96},{96,112},{112,128},... | collective-permute-start | bytes 49160 | tf_op jit(solution)/shard_map/while/body/eval_jaxpr/ppermute | solution.py:20
  271.2 14.8 %all-to-all-start = ((bf16[32,16,384]{2,0,1:T(8,128)(2,1)}), bf16[32,16,384]{2,0,1:T(8,128)(2,1)S(1)}, u32[]{:S(2)}, u32[]{:S(2)}) async-start(bf16[32,16,384]{2,0,1:T(8,128)(2,1)} %reshape.201), calls=%async_computation | async-start | bytes 786432 | tf_op jit(solution)/shard_map/while/body/eval_jaxpr/all_to_all | solution.py:86
  287.2 23.4 %collective-permute-start = (bf16[8,1024]{1,0:T(8,128)(2,1)S(1)}, bf16[8,1024]{1,0:T(8,128)(2,1)S(1)}, u32[]{:S(2)}, u32[]{:S(2)}) collective-permute-start(bf16[8,1024]{1,0:T(8,128)(2,1)S(1)} %copy.55), channel_id=1, source_target_pairs={{0,16},{16,32},{32,48},{48,64},{64,80},{80,96},{96,112},{112,128},... | collective-permute-start | bytes 49160 | tf_op jit(solution)/shard_map/while/body/eval_jaxpr/ppermute | solution.py:20
  294.9 14.8 %all-to-all-start = ((bf16[32,16,384]{2,0,1:T(8,128)(2,1)}), bf16[32,16,384]{2,0,1:T(8,128)(2,1)S(1)}, u32[]{:S(2)}, u32[]{:S(2)}) async-start(bf16[32,16,384]{2,0,1:T(8,128)(2,1)} %reshape.201), calls=%async_computation | async-start | bytes 786432 | tf_op jit(solution)/shard_map/while/body/eval_jaxpr/all_to_all | solution.py:86
  310.9 23.4 %collective-permute-start = (bf16[8,1024]{1,0:T(8,128)(2,1)S(1)}, bf16[8,1024]{1,0:T(8,128)(2,1)S(1)}, u32[]{:S(2)}, u32[]{:S(2)}) collective-permute-start(bf16[8,1024]{1,0:T(8,128)(2,1)S(1)} %copy.55), channel_id=1, source_target_pairs={{0,16},{16,32},{32,48},{48,64},{64,80},{80,96},{96,112},{112,128},... | collective-permute-start | bytes 49160 | tf_op jit(solution)/shard_map/while/body/eval_jaxpr/ppermute | solution.py:20
  318.7 14.8 %all-to-all-start = ((bf16[32,16,384]{2,0,1:T(8,128)(2,1)}), bf16[32,16,384]{2,0,1:T(8,128)(2,1)S(1)}, u32[]{:S(2)}, u32[]{:S(2)}) async-start(bf16[32,16,384]{2,0,1:T(8,128)(2,1)} %reshape.201), calls=%async_computation | async-start | bytes 786432 | tf_op jit(solution)/shard_map/while/body/eval_jaxpr/all_to_all | solution.py:86
  334.7 22.9 %collective-permute-start = (bf16[8,1024]{1,0:T(8,128)(2,1)S(1)}, bf16[8,1024]{1,0:T(8,128)(2,1)S(1)}, u32[]{:S(2)}, u32[]{:S(2)}) collective-permute-start(bf16[8,1024]{1,0:T(8,128)(2,1)S(1)} %copy.55), channel_id=1, source_target_pairs={{0,16},{16,32},{32,48},{48,64},{64,80},{80,96},{96,112},{112,128},... | collective-permute-start | bytes 49160 | tf_op jit(solution)/shard_map/while/body/eval_jaxpr/ppermute | solution.py:20
  357.7 24.3 %collective-permute-start = (bf16[8,1024]{1,0:T(8,128)(2,1)S(1)}, bf16[8,1024]{1,0:T(8,128)(2,1)S(1)}, u32[]{:S(2)}, u32[]{:S(2)}) collective-permute-start(bf16[8,1024]{1,0:T(8,128)(2,1)S(1)} %copy.55), channel_id=1, source_target_pairs={{0,16},{16,32},{32,48},{48,64},{64,80},{80,96},{96,112},{112,128},... | collective-permute-start | bytes 49160 | tf_op jit(solution)/shard_map/while/body/eval_jaxpr/ppermute | solution.py:20
  366.3 14.8 %all-to-all-start = ((bf16[32,16,384]{2,0,1:T(8,128)(2,1)}), bf16[32,16,384]{2,0,1:T(8,128)(2,1)S(1)}, u32[]{:S(2)}, u32[]{:S(2)}) async-start(bf16[32,16,384]{2,0,1:T(8,128)(2,1)} %reshape.201), calls=%async_computation | async-start | bytes 786432 | tf_op jit(solution)/shard_map/while/body/eval_jaxpr/all_to_all | solution.py:86
  382.3 24.3 %collective-permute-start = (bf16[8,1024]{1,0:T(8,128)(2,1)S(1)}, bf16[8,1024]{1,0:T(8,128)(2,1)S(1)}, u32[]{:S(2)}, u32[]{:S(2)}) collective-permute-start(bf16[8,1024]{1,0:T(8,128)(2,1)S(1)} %copy.55), channel_id=1, source_target_pairs={{0,16},{16,32},{32,48},{48,64},{64,80},{80,96},{96,112},{112,128},... | collective-permute-start | bytes 49160 | tf_op jit(solution)/shard_map/while/body/eval_jaxpr/ppermute | solution.py:20
  391.0 14.8 %all-to-all-start = ((bf16[32,16,384]{2,0,1:T(8,128)(2,1)}), bf16[32,16,384]{2,0,1:T(8,128)(2,1)S(1)}, u32[]{:S(2)}, u32[]{:S(2)}) async-start(bf16[32,16,384]{2,0,1:T(8,128)(2,1)} %reshape.201), calls=%async_computation | async-start | bytes 786432 | tf_op jit(solution)/shard_map/while/body/eval_jaxpr/all_to_all | solution.py:86
  406.9 24.3 %collective-permute-start = (bf16[8,1024]{1,0:T(8,128)(2,1)S(1)}, bf16[8,1024]{1,0:T(8,128)(2,1)S(1)}, u32[]{:S(2)}, u32[]{:S(2)}) collective-permute-start(bf16[8,1024]{1,0:T(8,128)(2,1)S(1)} %copy.55), channel_id=1, source_target_pairs={{0,16},{16,32},{32,48},{48,64},{64,80},{80,96},{96,112},{112,128},... | collective-permute-start | bytes 49160 | tf_op jit(solution)/shard_map/while/body/eval_jaxpr/ppermute | solution.py:20
  415.6 14.8 %all-to-all-start = ((bf16[32,16,384]{2,0,1:T(8,128)(2,1)}), bf16[32,16,384]{2,0,1:T(8,128)(2,1)S(1)}, u32[]{:S(2)}, u32[]{:S(2)}) async-start(bf16[32,16,384]{2,0,1:T(8,128)(2,1)} %reshape.201), calls=%async_computation | async-start | bytes 786432 | tf_op jit(solution)/shard_map/while/body/eval_jaxpr/all_to_all | solution.py:86
  431.2 15.2 %collective-permute-start.1 = (bf16[8]{0:T(256)(128)(2,1)S(1)}, bf16[8]{0:T(256)(128)(2,1)S(1)}, u32[]{:S(2)}, u32[]{:S(2)}) collective-permute-start(bf16[8]{0:T(256)(128)(2,1)S(1)} %convert_element_type.257), channel_id=1, source_target_pairs={{0,16},{16,32},{32,48},{48,64},{64,80},{80,96},{96,112},{112,128},... | collective-permute-start | bytes 56 | tf_op jit(solution)/shard_map/while/body/eval_jaxpr/ppermute | solution.py:20
  431.5 25.5 %collective-permute-start = (bf16[8,1024]{1,0:T(8,128)(2,1)S(1)}, bf16[8,1024]{1,0:T(8,128)(2,1)S(1)}, u32[]{:S(2)}, u32[]{:S(2)}) collective-permute-start(bf16[8,1024]{1,0:T(8,128)(2,1)S(1)} %copy.55), channel_id=1, source_target_pairs={{0,16},{16,32},{32,48},{48,64},{64,80},{80,96},{96,112},{112,128},... | collective-permute-start | bytes 49160 | tf_op jit(solution)/shard_map/while/body/eval_jaxpr/ppermute | solution.py:20
  441.4 14.8 %all-to-all-start = ((bf16[32,16,384]{2,0,1:T(8,128)(2,1)}), bf16[32,16,384]{2,0,1:T(8,128)(2,1)S(1)}, u32[]{:S(2)}, u32[]{:S(2)}) async-start(bf16[32,16,384]{2,0,1:T(8,128)(2,1)} %reshape.201), calls=%async_computation | async-start | bytes 786432 | tf_op jit(solution)/shard_map/while/body/eval_jaxpr/all_to_all | solution.py:86
  457.4 23.4 %collective-permute-start = (bf16[8,1024]{1,0:T(8,128)(2,1)S(1)}, bf16[8,1024]{1,0:T(8,128)(2,1)S(1)}, u32[]{:S(2)}, u32[]{:S(2)}) collective-permute-start(bf16[8,1024]{1,0:T(8,128)(2,1)S(1)} %copy.55), channel_id=1, source_target_pairs={{0,16},{16,32},{32,48},{48,64},{64,80},{80,96},{96,112},{112,128},... | collective-permute-start | bytes 49160 | tf_op jit(solution)/shard_map/while/body/eval_jaxpr/ppermute | solution.py:20
  465.2 14.8 %all-to-all-start = ((bf16[32,16,384]{2,0,1:T(8,128)(2,1)}), bf16[32,16,384]{2,0,1:T(8,128)(2,1)S(1)}, u32[]{:S(2)}, u32[]{:S(2)}) async-start(bf16[32,16,384]{2,0,1:T(8,128)(2,1)} %reshape.201), calls=%async_computation | async-start | bytes 786432 | tf_op jit(solution)/shard_map/while/body/eval_jaxpr/all_to_all | solution.py:86
  481.2 23.4 %collective-permute-start = (bf16[8,1024]{1,0:T(8,128)(2,1)S(1)}, bf16[8,1024]{1,0:T(8,128)(2,1)S(1)}, u32[]{:S(2)}, u32[]{:S(2)}) collective-permute-start(bf16[8,1024]{1,0:T(8,128)(2,1)S(1)} %copy.55), channel_id=1, source_target_pairs={{0,16},{16,32},{32,48},{48,64},{64,80},{80,96},{96,112},{112,128},... | collective-permute-start | bytes 49160 | tf_op jit(solution)/shard_map/while/body/eval_jaxpr/ppermute | solution.py:20
  504.9 23.4 %collective-permute-start = (bf16[8,1024]{1,0:T(8,128)(2,1)S(1)}, bf16[8,1024]{1,0:T(8,128)(2,1)S(1)}, u32[]{:S(2)}, u32[]{:S(2)}) collective-permute-start(bf16[8,1024]{1,0:T(8,128)(2,1)S(1)} %copy.55), channel_id=1, source_target_pairs={{0,16},{16,32},{32,48},{48,64},{64,80},{80,96},{96,112},{112,128},... | collective-permute-start | bytes 49160 | tf_op jit(solution)/shard_map/while/body/eval_jaxpr/ppermute | solution.py:20
  512.7 14.8 %all-to-all-start = ((bf16[32,16,384]{2,0,1:T(8,128)(2,1)}), bf16[32,16,384]{2,0,1:T(8,128)(2,1)S(1)}, u32[]{:S(2)}, u32[]{:S(2)}) async-start(bf16[32,16,384]{2,0,1:T(8,128)(2,1)} %reshape.201), calls=%async_computation | async-start | bytes 786432 | tf_op jit(solution)/shard_map/while/body/eval_jaxpr/all_to_all | solution.py:86
  539.1 154.1 %reduce-scatter.2.cloned.1.call-start = ((), (), s32[]{:S(2)}) async-start(), calls=%async_computation.4 | async-start | bytes 6684672 | tf_op jit(solution)/shard_map/reduce_scatter | solution.py:31
  (20 other events, 686.2 us)
Sparse Core Ops, SparseCore 0:
  10.0 147.3 all-reduce.1
  557.4 135.6 reduce-scatter.1
where the time goes:
time: 702 us; the launch traced here: 700 us
  waiting for transfers between devices  437 us (62%)
  starting transfers between devices  109 us (16%)
  matrix products  89.2 us (13%)
  local copies, waits for them, and re-layouts  43.6 us (6%)
  between operations  13.5 us (2%)
    all_to_all x16, waiting for transfers between devices, project_band(): lax.all_to_all(outgoing, 'gblk', split_axis=1, concat_axis=1, tiled=True)  156 us
    psum x1, waiting for transfers between devices, spread(): return lax.psum(block, axis)  146 us
    reduce_scatter x1, waiting for transfers between devices, band_reduce(): lax.psum_scatter(partial_rows, 'band', scatter_dimension=1, tiled=True)  136 us
    all_to_all x16, starting transfers between devices, project_band(): lax.all_to_all(outgoing, 'gblk', split_axis=1, concat_axis=1, tiled=True)  76.9 us
    dot_general x16, matrix products, project_band(): jnp.dot(pair_rows, sphere_basis, preferred_element_type=jnp.float32)  74.9 us
    ppermute x30, starting transfers between devices, from_behind(): return lax.ppermute(value, axis, pairs)  32.3 us
    reshape x32, local copies, waits for them, and re-layouts, project_band(): outgoing.astype(jnp.bfloat16)  21.4 us
  transfers between devices with their start and end apart: 48, of which 18 were waited for; matrix products, arithmetic and copies ran while one was open for 17% of the time, Pallas kernels for 0%

commit v1 on v0

v1 whole, which is shorter than its diff:
```python
import functools
import math

import jax
import jax.numpy as jnp
from jax import lax
from jax.experimental import pallas as pl
from jax.experimental.pallas import tpu as pltpu
from jax.sharding import PartitionSpec as P

BLK = 128
CAP = 3
GROUP = 16
VAL = 8
CON = 4

f32 = jnp.float32
bf16 = jnp.bfloat16


def band_order(n):
    def hops(d):
        z = (d // 2) % 8
        return min(z, 8 - z) + d % 2

    return sorted(range(1, n), key=lambda d: -hops(d))


def gblk_order(n):
    def hops(d):
        x = d // 4
        return min(x, 4 - x) + 2 * ((d // 2) % 2) + d % 2

    return sorted(range(1, n), key=lambda d: -hops(d))


def kernel(
    nb,
    ng,
    factor,
    val_hbm,
    con_hbm,
    ve_ref,
    ce_ref,
    owner_ref,
    fill_ref,
    table_hbm,
    out_ref,
    val_v,
    con_v,
    table_v,
    win_v,
    psi,
    turned,
    bw,
    con_f,
    x_s,
    s_s,
    m_s,
    chi,
    send,
    slot_s,
    ld_sem,
    gs_sem,
    gr_sem,
    fs_sem,
    fr_sem,
    ws_sem,
    wr_sem,
    cs_sem,
    cr_sem,
    own_sem,
):
    b = lax.axis_index("band")
    p = lax.axis_index("gblk")
    core = lax.rem(p, 2)
    partner = p + 1 - 2 * core
    r = psi.shape[1]
    half = r // 2
    cols = table_v.shape[1]
    blocks = cols // BLK
    border = band_order(nb)
    gorder = gblk_order(ng)

    barrier = pltpu.get_barrier_semaphore()
    for d in border:
        pl.semaphore_signal(barrier, 1, device_id={"band": lax.rem(b + d, nb)})
    for d in gorder:
        pl.semaphore_signal(barrier, 1, device_id={"gblk": lax.rem(p + d, ng)})

    ld_val = pltpu.make_async_copy(val_hbm, val_v, ld_sem.at[0])
    ld_con = pltpu.make_async_copy(con_hbm, con_v, ld_sem.at[1])
    ld_val.start()
    ld_con.start()
    wcol = pl.multiple_of((b // 8) * BLK, BLK)

    def win_copy():
        return pltpu.make_async_copy(
            table_hbm.at[:, pl.ds(wcol, BLK)], win_v, ld_sem.at[3]
        )

    @pl.when(p == 0)
    def _():
        win_copy().start()

    ld_table = pltpu.make_async_copy(table_hbm, table_v, ld_sem.at[2])
    ld_table.start()

    lane = lax.broadcasted_iota(jnp.int32, (1, 256), 1)
    energy = jnp.zeros((1, 256), f32)
    for j in range(VAL):
        energy = jnp.where(lane % GROUP == j, ve_ref[j], energy)
    for j in range(CON):
        energy = jnp.where(lane % GROUP == VAL + j, ce_ref[j], energy)
    hi = energy.astype(bf16).astype(f32)
    mid = (energy - hi).astype(bf16).astype(f32)
    lo = energy - hi - mid
    parts = jnp.concatenate([hi, mid, lo, jnp.zeros_like(hi)], axis=0)
    parts = jnp.concatenate([parts, jnp.zeros((4, r - 256), f32)], axis=1)
    ld_val.wait()
    ld_con.wait()
    mine = jnp.concatenate([val_v[...].astype(f32), con_v[...].astype(f32), parts], axis=0)
    my_rows = pl.ds(pl.multiple_of(b * GROUP, GROUP), GROUP)
    psi[my_rows, :] = mine.astype(bf16)

    @pl.when(p == 0)
    def _():
        win_copy().wait()
        turned[...] = win_v[...].astype(f32).T
        bw[...] = turned[pl.ds(pl.multiple_of(lax.rem(b, 8) * 16, 16), 16), :].astype(bf16)

    pl.semaphore_wait(barrier, nb + ng - 2)

    my_cols = pl.ds(pl.multiple_of(core * half, half), half)

    def gather_copy(i, group):
        rows = pl.ds(pl.multiple_of(group * GROUP, GROUP), GROUP)
        return pltpu.make_async_remote_copy(
            src_ref=psi.at[rows, my_cols],
            dst_ref=psi.at[rows, my_cols],
            send_sem=gs_sem.at[i],
            recv_sem=gr_sem.at[i],
            device_id={"band": lax.rem(b + border[i], nb)},
        )

    def window_copy(d):
        return pltpu.make_async_remote_copy(
            src_ref=bw,
            dst_ref=bw,
            send_sem=ws_sem.at[d],
            recv_sem=wr_sem,
            device_id={"gblk": d},
        )

    def window_forward():
        return pltpu.make_async_remote_copy(
            src_ref=bw,
            dst_ref=bw,
            send_sem=ws_sem.at[0],
            recv_sem=wr_sem,
            device_id={"gblk": partner},
        )

    @pl.when(p == 0)
    def _():
        for d in range(ng - 2, 0, -2):
            window_copy(d).start()
        window_copy(1).start()

    for i in range(nb - 1):
        gather_copy(i, b).start()

    def slots_of(o, carry):
        count = jnp.int32(0)
        first = jnp.int32(blocks)
        second = jnp.int32(blocks)
        third = jnp.int32(blocks)
        for j in range(blocks):
            hit = owner_ref[p * blocks + j] == o
            first = jnp.where(hit & (count == 0), j, first)
            second = jnp.where(hit & (count == 1), j, second)
            third = jnp.where(hit & (count == 2), j, third)
            count = count + jnp.where(hit, 1, 0)
        slot_s[o * CAP] = first
        slot_s[o * CAP + 1] = second
        slot_s[o * CAP + 2] = third
        return carry

    lax.fori_loop(0, ng, slots_of, 0)
    chi[blocks] = jnp.zeros((GROUP, BLK), bf16)

    def forward_copy(i, group):
        rows = pl.ds(pl.multiple_of(group * GROUP, GROUP), GROUP)
        return pltpu.make_async_remote_copy(
            src_ref=psi.at[rows, my_cols],
            dst_ref=psi.at[rows, my_cols],
            send_sem=fs_sem.at[i],
            recv_sem=fr_sem.at[i],
            device_id={"gblk": partner},
        )

    for i in reversed(range(nb - 1)):
        source = lax.rem(b + nb - border[i], nb)
        gather_copy(i, source).wait_recv()
        forward_copy(i, source).start()

    @pl.when(p > 0)
    def _():
        window_forward().wait_recv()

    @pl.when((core == 0) & (p > 0))
    def _():
        window_forward().start()

    for i in reversed(range(nb - 1)):
        source = lax.rem(b + nb - border[i], nb)
        forward_copy(i, source).wait_recv()

    rows_n = nb * GROUP
    cons = nb * CON
    glane = lax.broadcasted_iota(jnp.int32, (GROUP, rows_n), 1)
    on_lanes = jnp.zeros((1, rows_n), f32)
    for g in range(nb):
        tile = psi[g * GROUP : (g + 1) * GROUP, 0:rows_n].astype(f32)
        grow = lax.broadcasted_iota(jnp.int32, (GROUP, rows_n), 0)
        keep = (glane // GROUP == g) & (grow >= 12) & (grow < 15)
        on_lanes = on_lanes + jnp.sum(jnp.where(keep, tile, 0.0), axis=0, keepdims=True)
    clane = lax.broadcasted_iota(jnp.int32, (cons, rows_n), 1)
    crow = lax.broadcasted_iota(jnp.int32, (cons, rows_n), 0)
    pick = clane == (crow // CON) * GROUP + VAL + crow % CON
    on_rows = jnp.sum(jnp.where(pick, on_lanes, 0.0), axis=1, keepdims=True)
    is_val = clane % GROUP < VAL
    gap = jnp.where(is_val, on_lanes - on_rows, -1.0)
    weight = jnp.where(is_val, factor / gap, 0.0)

    for g in range(0, nb, 2):
        one = psi[g * GROUP : (g + 1) * GROUP, :].astype(f32)[VAL : VAL + CON]
        two = psi[(g + 1) * GROUP : (g + 2) * GROUP, :].astype(f32)[VAL : VAL + CON]
        con_f[g * CON : (g + 2) * CON, :] = jnp.concatenate([one, two], axis=0)

    wrow = lax.broadcasted_iota(jnp.int32, (16, 1), 0) + lax.rem(b, 8) * 16
    win_live = (wrow < fill_ref[b // 8]).astype(f32)
    window = bw[...].astype(f32) * win_live
    for h in range(16):
        x_s[h * cons : (h + 1) * cons, :] = (con_f[...] * window[h : h + 1, :]).astype(bf16)

    group_h = 4
    rows_h = group_h * cons
    weight_t = jnp.concatenate([weight] * group_h, axis=0)
    for q in range(16 // group_h):
        chunk = slice(q * rows_h, (q + 1) * rows_h)
        raw = lax.dot_general(
            x_s[chunk, :], psi[...], (((1,), (1,)), ((), ())), preferred_element_type=f32
        )
        s_s[chunk, :] = (raw * weight_t).astype(bf16)
    for q in range(16 // group_h):
        chunk = slice(q * rows_h, (q + 1) * rows_h)
        full = jnp.dot(s_s[chunk, :], psi[...], preferred_element_type=f32)
        for i in range(group_h):
            part = full[i * cons : (i + 1) * cons, :] * con_f[...]
            h = q * group_h + i
            m_s[h : h + 1, :] = jnp.sum(part, axis=0, keepdims=True)

    m_hi = m_s[...].astype(bf16)
    m_lo = (m_s[...] - m_hi.astype(f32)).astype(bf16)
    m_two = jnp.concatenate([m_hi, m_lo], axis=0)

    ld_table.wait()
    lanes = lax.broadcasted_iota(jnp.int32, (1, BLK), 1)
    step = 6
    for n in range(0, blocks, step):
        wide = jnp.dot(
            m_two, table_v[:, n * BLK : (n + step) * BLK], preferred_element_type=f32
        )
        wide = wide[0:16] + wide[16:32]
        for j in range(step):
            live = (lanes < fill_ref[p * blocks + n + j]).astype(f32)
            chi[n + j] = (wide[:, j * BLK : (j + 1) * BLK] * live).astype(bf16)

    my_slots = pl.ds(pl.multiple_of(p * CAP * BLK, CAP * BLK), CAP * BLK)

    def fill_slots(o):
        for s in range(CAP):
            send[o, :, s * BLK : (s + 1) * BLK] = chi[slot_s[o * CAP + s]]

    def owner_copy(i):
        o = lax.rem(p + gorder[i], ng)
        return pltpu.make_async_remote_copy(
            src_ref=send.at[o],
            dst_ref=out_ref.at[:, my_slots],
            send_sem=cs_sem.at[i],
            recv_sem=cr_sem.at[i],
            device_id={"gblk": o},
        )

    for i in range(ng - 1):
        fill_slots(lax.rem(p + gorder[i], ng))
        owner_copy(i).start()
    fill_slots(p)
    own = pltpu.make_async_copy(send.at[p], out_ref.at[:, my_slots], own_sem)
    own.start()

    for i in range(nb - 1):
        source = lax.rem(b + nb - border[i], nb)
        gather_copy(i, b).wait_send()
        forward_copy(i, source).wait_send()

    @pl.when(p == 0)
    def _():
        for d in range(ng - 2, 0, -2):
            window_copy(d).wait_send()
        window_copy(1).wait_send()

    @pl.when((core == 0) & (p > 0))
    def _():
        window_forward().wait_send()

    own.wait()
    for i in range(ng - 1):
        o = lax.rem(p + ng - gorder[i], ng)
        from_slots = pl.ds(pl.multiple_of(o * CAP * BLK, CAP * BLK), CAP * BLK)
        owner_copy(i).wait_send()
        pltpu.make_async_remote_copy(
            src_ref=send.at[o],
            dst_ref=out_ref.at[:, from_slots],
            send_sem=cs_sem.at[i],
            recv_sem=cr_sem.at[i],
            device_id={"gblk": o},
        ).wait_recv()


def per_device(nb, ng, psi_val, psi_con, val_energy, con_energy, sphere_basis, block_owner, block_fill):
    r, cols = sphere_basis.shape
    blocks = cols // BLK
    factor = 1.0 / math.sqrt(psi_val.shape[0] * nb * psi_con.shape[0] * nb)
    any_spec = pl.BlockSpec(memory_space=pl.ANY)
    smem = pl.BlockSpec(memory_space=pltpu.SMEM)
    slot_cols = ng * CAP * BLK
    dma = pltpu.SemaphoreType.DMA
    got = pl.pallas_call(
        functools.partial(kernel, nb, ng, factor),
        out_shape=jax.ShapeDtypeStruct((16, slot_cols), bf16),
        in_specs=[any_spec, any_spec, smem, smem, smem, smem, any_spec],
        out_specs=any_spec,
        scratch_shapes=[
            pltpu.VMEM((VAL, r), bf16),
            pltpu.VMEM((CON, r), bf16),
            pltpu.VMEM((r, cols), bf16),
            pltpu.VMEM((r, BLK), bf16),
            pltpu.VMEM((nb * GROUP, r), bf16),
            pltpu.VMEM((BLK, r), f32),
            pltpu.VMEM((16, r), bf16),
            pltpu.VMEM((nb * CON, r), f32),
            pltpu.VMEM((16 * nb * CON, r), bf16),
            pltpu.VMEM((16 * nb * CON, nb * GROUP), bf16),
            pltpu.VMEM((16, r), f32),
            pltpu.VMEM((blocks + 1, 16, BLK), bf16),
            pltpu.VMEM((ng, 16, CAP * BLK), bf16),
            pltpu.SMEM((ng * CAP,), jnp.int32),
            dma((4,)),
            dma((nb - 1,)),
            dma((nb - 1,)),
            dma((nb - 1,)),
            dma((nb - 1,)),
            dma((ng,)),
            dma(()),
            dma((ng - 1,)),
            dma((ng - 1,)),
            dma(()),
        ],
        name="polarizability",
        compiler_params=pltpu.CompilerParams(
            collective_id=0, has_side_effects=True, vmem_limit_bytes=48 * 1024 * 1024
        ),
    )(psi_val, psi_con, val_energy, con_energy, block_owner, block_fill, sphere_basis)
    return got.astype(f32).T


def solution(mesh):
    nb, ng = mesh.shape["band"], mesh.shape["gblk"]
    return jax.shard_map(
        functools.partial(per_device, nb, ng),
        mesh=mesh,
        in_specs=(
            P("band", None),
            P("band", None),
            P("band"),
            P("band"),
            P(None, "gblk"),
            P(),
            P(),
        ),
        out_specs=P("gblk", "band"),
        check_vma=False,
    )
```

time: 702 us -> 34.4 us (0.05)
  waiting for transfers between devices: 437 us -> 0 us
  starting transfers between devices: 109 us -> 0 us
  matrix products: 89.2 us -> 0 us
  local copies, waits for them, and re-layouts: 43.6 us -> 4.08 us
  Pallas kernels: 0 us -> 29.3 us
  between operations: 13.5 us -> 0.02 us
    all_to_all x16 -> x0, waiting for transfers between devices: 156 us -> none  [project_band(): lax.all_to_all(outgoing, 'gblk', split_axis=1, concat_axis=1, tiled=True)]
    psum x1 -> x0, waiting for transfers between devices: 146 us -> none  [spread(): return lax.psum(block, axis)]
    reduce_scatter x1 -> x0, waiting for transfers between devices: 136 us -> none  [band_reduce(): lax.psum_scatter(partial_rows, 'band', scatter_dimension=1, tiled=True)]
    dot_general x49 -> x0, matrix products: 89.2 us -> none  [the longest x16 74.9 us: project_band(): jnp.dot(pair_rows, sphere_basis, preferred_element_type=jnp.float32)]
    all_to_all x16 -> x0, starting transfers between devices: 76.9 us -> none  [project_band(): lax.all_to_all(outgoing, 'gblk', split_axis=1, concat_axis=1, tiled=True)]
    ppermute x30 -> x0, starting transfers between devices: 32.3 us -> none  [from_behind(): return lax.ppermute(value, axis, pairs)]
    pallas_call x0 -> x1, Pallas kernels: none -> 29.3 us  [per_device(): pl.pallas_call(functools.partial(kernel, nb, ng, factor), out_shape=jax.S...]
    reshape x66 -> x0, local copies, waits for them, and re-layouts: 25.6 us -> none  [the longest x32 21.4 us: project_band(): outgoing.astype(jnp.bfloat16)]
  transfers between devices with their start and end apart: 48 -> 0, of which waited for: 18 -> 0; matrix products, arithmetic and copies ran while one was open for 17% -> 0% of each run, Pallas kernels for 0% -> 0%
where the time goes in v1:
time: 34.4 us; the launch traced here: 34.2 us
  Pallas kernels  29.3 us (85%)
  local copies, waits for them, and re-layouts  4.08 us (12%)
  other arithmetic  0.77 us (2%)
    pallas_call x1, Pallas kernels, per_device(): pl.pallas_call(functools.partial(kernel, nb, ng, factor), out_shape=jax.S...  29.3 us
    unnamed x12, local copies, waits for them, and re-layouts  4.08 us
    transpose x1, other arithmetic, per_device(): return got.astype(f32).T  0.77 us

profile of v1, /device:TPU:1, one launch (start us, length us, event | category | flops | bytes accessed | tf_op | source)
XLA Modules:
  0.0 34.2 jit_solution(7737185270251835038)
XLA Ops:
  0.0 0.0 copy-start
  0.0 0.7 %copy-done = bf16[8,1024]{1,0:T(8,128)(2,1)S(1)} copy-done((bf16[8,1024]{1,0:T(8,128)(2,1)S(1)}, bf16[8,1024]{1,0:T(8,128)(2,1)}, u32[]{:S(2)}) %copy-start) | copy-done | bytes 16408
  0.7 0.0 copy-start.1
  0.7 0.7 %copy-done.1 = bf16[4,1024]{1,0:T(4,128)(2,1)S(1)} copy-done((bf16[4,1024]{1,0:T(4,128)(2,1)S(1)}, bf16[4,1024]{1,0:T(4,128)(2,1)}, u32[]{:S(2)}) %copy-start.1) | copy-done | bytes 8216
  1.4 0.0 copy-start.2
  1.4 0.7 %copy-done.2 = s32[480]{0:T(512)S(1)} copy-done((s32[480]{0:T(512)S(1)}, s32[480]{0:T(512)}, u32[]{:S(2)}) %copy-start.2) | copy-done | bytes 1944
  2.1 0.0 copy-start.3
  2.1 0.7 %copy-done.3 = s32[480]{0:T(512)S(1)} copy-done((s32[480]{0:T(512)S(1)}, s32[480]{0:T(512)}, u32[]{:S(2)}) %copy-start.3) | copy-done | bytes 1944
  2.8 0.0 copy-start.4
  2.8 0.7 %copy-done.4 = f32[8]{0:T(128)S(1)} copy-done((f32[8]{0:T(128)S(1)}, f32[8]{0:T(128)}, u32[]{:S(2)}) %copy-start.4) | copy-done | bytes 56
  3.4 0.0 copy-start.5
  3.4 0.7 %copy-done.5 = f32[4]{0:T(128)S(1)} copy-done((f32[4]{0:T(128)S(1)}, f32[4]{0:T(128)}, u32[]{:S(2)}) %copy-start.5) | copy-done | bytes 40
  4.1 29.3 %polarizability.1 = bf16[16,6144]{1,0:T(8,128)(2,1)S(1)} custom-call(bf16[8,1024]{1,0:T(8,128)(2,1)S(1)} %copy-done, bf16[4,1024]{1,0:T(4,128)(2,1)S(1)} %copy-done.1, f32[8]{0:T(128)S(1)} %copy-done.4, f32[4]{0:T(128)S(1)} %copy-done.5, s32[480]{0:T(512)S(1)} %copy-done.2, s32[480]{0:T(512)S(1)} %copy-done.3, bf16[1024,3840]{1,0:T(8,128)(2,1)} %table_hbm.1), custom_call_target="tpu_custom_call" | custom-call | tf_op jit(solution)/shard_map/polarizability/pallas_call | solution.py:340
  33.4 0.8 %convert_bitcast_fusion = f32[6144,16]{0,1:T(8,128)} fusion(bf16[16,6144]{1,0:T(8,128)(2,1)S(1)} %polarizability.1), kind=kLoop, calls=%fused_computation | loop fusion | flops 98304 | bytes 589824 | tf_op jit(solution)/shard_map/transpose | solution.py:376
Async XLA Ops:
  0.0 0.7 %copy-start = (bf16[8,1024]{1,0:T(8,128)(2,1)S(1)}, bf16[8,1024]{1,0:T(8,128)(2,1)}, u32[]{:S(2)}) copy-start(bf16[8,1024]{1,0:T(8,128)(2,1)} %val_hbm.1) | copy-start | bytes 49156
  0.7 0.7 %copy-start.1 = (bf16[4,1024]{1,0:T(4,128)(2,1)S(1)}, bf16[4,1024]{1,0:T(4,128)(2,1)}, u32[]{:S(2)}) copy-start(bf16[4,1024]{1,0:T(4,128)(2,1)} %con_hbm.1) | copy-start | bytes 24580
  1.4 0.7 %copy-start.2 = (s32[480]{0:T(512)S(1)}, s32[480]{0:T(512)}, u32[]{:S(2)}) copy-start(s32[480]{0:T(512)} %owner_ref.1) | copy-start | bytes 5764
  2.1 0.7 %copy-start.3 = (s32[480]{0:T(512)S(1)}, s32[480]{0:T(512)}, u32[]{:S(2)}) copy-start(s32[480]{0:T(512)} %fill_ref.1) | copy-start | bytes 5764
  2.8 0.7 %copy-start.4 = (f32[8]{0:T(128)S(1)}, f32[8]{0:T(128)}, u32[]{:S(2)}) copy-start(f32[8]{0:T(128)} %ve_ref.1) | copy-start | bytes 100
  3.4 0.7 %copy-start.5 = (f32[4]{0:T(128)S(1)}, f32[4]{0:T(128)}, u32[]{:S(2)}) copy-start(f32[4]{0:T(128)} %ce_ref.1) | copy-start | bytes 52

commit v2 on v1

--- a/solution.py
+++ b/solution.py
@@ -40,12 +40,16 @@
     factor,
     val_hbm,
     con_hbm,
+    ve_hbm,
+    ce_hbm,
+    owner_hbm,
+    fill_hbm,
+    table_hbm,
+    out_ref,
     ve_ref,
     ce_ref,
     owner_ref,
     fill_ref,
-    table_hbm,
-    out_ref,
     val_v,
     con_v,
     table_v,
@@ -57,10 +61,10 @@
     x_s,
     s_s,
     m_s,
-    chi,
     send,
     slot_s,
     ld_sem,
+    tb_sem,
     gs_sem,
     gr_sem,
     fs_sem,
@@ -77,8 +81,7 @@
     partner = p + 1 - 2 * core
     r = psi.shape[1]
     half = r // 2
-    cols = table_v.shape[1]
-    blocks = cols // BLK
+    blocks = table_v.shape[0]
     border = band_order(nb)
     gorder = gblk_order(ng)
 
@@ -88,10 +91,14 @@
     for d in gorder:
         pl.semaphore_signal(barrier, 1, device_id={"gblk": lax.rem(p + d, ng)})
 
+    ld_ve = pltpu.make_async_copy(ve_hbm, ve_ref, ld_sem.at[4])
+    ld_ce = pltpu.make_async_copy(ce_hbm, ce_ref, ld_sem.at[5])
     ld_val = pltpu.make_async_copy(val_hbm, val_v, ld_sem.at[0])
     ld_con = pltpu.make_async_copy(con_hbm, con_v, ld_sem.at[1])
-    ld_val.start()
-    ld_con.start()
+    ld_owner = pltpu.make_async_copy(owner_hbm, owner_ref, ld_sem.at[6])
+    ld_fill = pltpu.make_async_copy(fill_hbm, fill_ref, ld_sem.at[7])
+    for load in (ld_ve, ld_ce, ld_val, ld_con):
+        load.start()
     wcol = pl.multiple_of((b // 8) * BLK, BLK)
 
     def win_copy():
@@ -103,11 +110,20 @@
     def _():
         win_copy().start()
 
-    ld_table = pltpu.make_async_copy(table_hbm, table_v, ld_sem.at[2])
-    ld_table.start()
+    def table_copy(j):
+        return pltpu.make_async_copy(
+            table_hbm.at[:, j * BLK : (j + 1) * BLK], table_v.at[j], tb_sem.at[j]
+        )
+
+    ld_owner.start()
+    ld_fill.start()
+    for j in range(blocks):
+        table_copy(j).start()
 
     lane = lax.broadcasted_iota(jnp.int32, (1, 256), 1)
     energy = jnp.zeros((1, 256), f32)
+    ld_ve.wait()
+    ld_ce.wait()
     for j in range(VAL):
         energy = jnp.where(lane % GROUP == j, ve_ref[j], energy)
     for j in range(CON):
@@ -186,8 +202,9 @@
         slot_s[o * CAP + 2] = third
         return carry
 
+    ld_owner.wait()
+    ld_fill.wait()
     lax.fori_loop(0, ng, slots_of, 0)
-    chi[blocks] = jnp.zeros((GROUP, BLK), bf16)
 
     def forward_copy(i, group):
         rows = pl.ds(pl.multiple_of(group * GROUP, GROUP), GROUP)
@@ -265,23 +282,21 @@
     m_lo = (m_s[...] - m_hi.astype(f32)).astype(bf16)
     m_two = jnp.concatenate([m_hi, m_lo], axis=0)
 
-    ld_table.wait()
-    lanes = lax.broadcasted_iota(jnp.int32, (1, BLK), 1)
-    step = 6
-    for n in range(0, blocks, step):
-        wide = jnp.dot(
-            m_two, table_v[:, n * BLK : (n + step) * BLK], preferred_element_type=f32
-        )
+    my_slots = pl.ds(pl.multiple_of(p * CAP * BLK, CAP * BLK), CAP * BLK)
+    lanes = lax.broadcasted_iota(jnp.int32, (1, CAP * BLK), 1)
+
+    def fill_slots(o):
+        table = []
+        limit = jnp.zeros((1, CAP * BLK), jnp.int32)
+        for s in range(CAP):
+            block = slot_s[o * CAP + s]
+            j = jnp.minimum(block, blocks - 1)
+            live = jnp.where(block < blocks, fill_ref[p * blocks + j], 0)
+            limit = jnp.where(lanes // BLK == s, live, limit)
+            table.append(table_v[j])
+        wide = jnp.dot(m_two, jnp.concatenate(table, axis=1), preferred_element_type=f32)
         wide = wide[0:16] + wide[16:32]
-        for j in range(step):
-            live = (lanes < fill_ref[p * blocks + n + j]).astype(f32)
-            chi[n + j] = (wide[:, j * BLK : (j + 1) * BLK] * live).astype(bf16)
-
-    my_slots = pl.ds(pl.multiple_of(p * CAP * BLK, CAP * BLK), CAP * BLK)
-
-    def fill_slots(o):
-        for s in range(CAP):
-            send[o, :, s * BLK : (s + 1) * BLK] = chi[slot_s[o * CAP + s]]
+        send[o] = jnp.where(lanes % BLK < limit, wide, 0.0).astype(bf16)
 
     def owner_copy(i):
         o = lax.rem(p + gorder[i], ng)
@@ -293,6 +308,8 @@
             device_id={"gblk": o},
         )
 
+    for j in range(blocks):
+        table_copy(j).wait()
     for i in range(ng - 1):
         fill_slots(lax.rem(p + gorder[i], ng))
         owner_copy(i).start()
@@ -333,19 +350,22 @@
     r, cols = sphere_basis.shape
     blocks = cols // BLK
     factor = 1.0 / math.sqrt(psi_val.shape[0] * nb * psi_con.shape[0] * nb)
-    any_spec = pl.BlockSpec(memory_space=pl.ANY)
-    smem = pl.BlockSpec(memory_space=pltpu.SMEM)
+    hbm = pl.BlockSpec(memory_space=pltpu.HBM)
     slot_cols = ng * CAP * BLK
     dma = pltpu.SemaphoreType.DMA
     got = pl.pallas_call(
         functools.partial(kernel, nb, ng, factor),
         out_shape=jax.ShapeDtypeStruct((16, slot_cols), bf16),
-        in_specs=[any_spec, any_spec, smem, smem, smem, smem, any_spec],
-        out_specs=any_spec,
+        in_specs=[hbm] * 7,
+        out_specs=pl.BlockSpec(memory_space=pl.ANY),
         scratch_shapes=[
+            pltpu.SMEM(val_energy.shape, f32),
+            pltpu.SMEM(con_energy.shape, f32),
+            pltpu.SMEM(block_owner.shape, jnp.int32),
+            pltpu.SMEM(block_fill.shape, jnp.int32),
             pltpu.VMEM((VAL, r), bf16),
             pltpu.VMEM((CON, r), bf16),
-            pltpu.VMEM((r, cols), bf16),
+            pltpu.VMEM((blocks, r, BLK), bf16),
             pltpu.VMEM((r, BLK), bf16),
             pltpu.VMEM((nb * GROUP, r), bf16),
             pltpu.VMEM((BLK, r), f32),
@@ -354,10 +374,10 @@
             pltpu.VMEM((16 * nb * CON, r), bf16),
             pltpu.VMEM((16 * nb * CON, nb * GROUP), bf16),
             pltpu.VMEM((16, r), f32),
-            pltpu.VMEM((blocks + 1, 16, BLK), bf16),
             pltpu.VMEM((ng, 16, CAP * BLK), bf16),
             pltpu.SMEM((ng * CAP,), jnp.int32),
-            dma((4,)),
+            dma((8,)),
+            dma((blocks,)),
             dma((nb - 1,)),
             dma((nb - 1,)),
             dma((nb - 1,)),
@@ -370,7 +390,7 @@
         ],
         name="polarizability",
         compiler_params=pltpu.CompilerParams(
-            collective_id=0, has_side_effects=True, vmem_limit_bytes=48 * 1024 * 1024
+            collective_id=0, has_side_effects=True, vmem_limit_bytes=60 * 1024 * 1024
         ),
     )(psi_val, psi_con, val_energy, con_energy, block_owner, block_fill, sphere_basis)
     return got.astype(f32).T

time: 34.4 us -> 32 us (0.930)
  local copies, waits for them, and re-layouts: 4.08 us -> 0 us
  other arithmetic: 0.77 us -> 1.7 us
  Pallas kernels: 29.3 us -> 30.1 us
    unnamed x12 -> x0, local copies, waits for them, and re-layouts: 4.08 us -> none
    transpose x1, other arithmetic: 0.77 us -> 1.7 us  [per_device(): return got.astype(f32).T]
    pallas_call x1, Pallas kernels: 29.3 us -> 30.1 us  [per_device(): pl.pallas_call(functools.partial(kernel, nb, ng, factor), out_shape=jax.S...]
where the time goes in v2:
time: 32 us; the launch traced here: 31.9 us
  Pallas kernels  30.1 us (94%)
  other arithmetic  1.7 us (5%)
    pallas_call x1, Pallas kernels, per_device(): pl.pallas_call(functools.partial(kernel, nb, ng, factor), out_shape=jax.S...  30.1 us
    transpose x1, other arithmetic, per_device(): return got.astype(f32).T  1.7 us

profile of v2, /device:TPU:1, one launch (start us, length us, event | category | flops | bytes accessed | tf_op | source)
XLA Modules:
  0.0 31.9 jit_solution(2941986979350571595)
XLA Ops:
  0.0 30.1 %polarizability.1 = bf16[16,6144]{1,0:T(8,128)(2,1)} custom-call(bf16[8,1024]{1,0:T(8,128)(2,1)} %val_hbm.1, bf16[4,1024]{1,0:T(4,128)(2,1)} %con_hbm.1, f32[8]{0:T(128)} %ve_hbm.1, f32[4]{0:T(128)} %ce_hbm.1, s32[480]{0:T(512)} %owner_hbm.1, s32[480]{0:T(512)} %fill_hbm.1, bf16[1024,3840]{1,0:T(8,128)(2,1)} %table_hbm.1), custom_call_target="tpu_custom_call" | custom-call | tf_op jit(solution)/shard_map/polarizability/pallas_call | solution.py:356
  30.2 1.7 %convert_bitcast_fusion = f32[6144,16]{0,1:T(8,128)} fusion(bf16[16,6144]{1,0:T(8,128)(2,1)} %polarizability.1), kind=kLoop, calls=%fused_computation | loop fusion | flops 98304 | bytes 589824 | tf_op jit(solution)/shard_map/transpose | solution.py:396

commit v3 on v2

v3 whole, which is shorter than its diff:
```python
import functools
import math

import jax
import jax.numpy as jnp
from jax import lax
from jax.experimental import pallas as pl
from jax.experimental.pallas import tpu as pltpu
from jax.sharding import PartitionSpec as P

BLK = 128
CAP = 3
GROUP = 16
VAL = 8
CON = 4
WIN = 16

f32 = jnp.float32
bf16 = jnp.bfloat16


def far_first(n, hops):
    return sorted(range(1, n), key=lambda d: -hops(d))


def band_hops(d):
    z = (d // 2) % 8
    return min(z, 8 - z) + d % 2


def gblk_hops(d):
    x = d // 4
    return min(x, 4 - x) + 2 * ((d // 2) % 2) + d % 2


def kernel(
    nb,
    ng,
    factor,
    val_hbm,
    con_hbm,
    ve_hbm,
    ce_hbm,
    owner_hbm,
    fill_hbm,
    table_hbm,
    out_ref,
    ve_ref,
    ce_ref,
    owner_ref,
    fill_ref,
    val_v,
    con_v,
    table_v,
    win_v,
    packed,
    energy,
    turned,
    bw,
    val_m,
    con_f,
    x_s,
    s_s,
    m_s,
    chi,
    send,
    slot_s,
    ld_sem,
    tb_sem,
    gs_sem,
    gr_sem,
    fs_sem,
    fr_sem,
    es_sem,
    er_sem,
    ws_sem,
    wr_sem,
    cs_sem,
    cr_sem,
    own_sem,
):
    b = lax.axis_index("band")
    p = lax.axis_index("gblk")
    core = lax.rem(p, 2)
    partner = p + 1 - 2 * core
    r = val_v.shape[1]
    vals, cons = nb * VAL, nb * CON
    val_cols, con_cols = r * VAL // GROUP, r * CON // GROUP
    blocks = table_v.shape[1] // BLK
    pairs = nb // 2
    border = far_first(nb, band_hops)
    gorder = far_first(ng, gblk_hops)
    steps = sorted(range(pairs), key=lambda i: -min(i, pairs - i))

    barrier = pltpu.get_barrier_semaphore()
    for d in border:
        pl.semaphore_signal(barrier, 1, device_id={"band": lax.rem(b + d, nb)})
    for d in gorder:
        pl.semaphore_signal(barrier, 1, device_id={"gblk": lax.rem(p + d, ng)})

    ld_val = pltpu.make_async_copy(val_hbm, val_v, ld_sem.at[0])
    ld_con = pltpu.make_async_copy(con_hbm, con_v, ld_sem.at[1])
    ld_ve = pltpu.make_async_copy(ve_hbm, ve_ref, ld_sem.at[2])
    ld_ce = pltpu.make_async_copy(ce_hbm, ce_ref, ld_sem.at[3])
    ld_owner = pltpu.make_async_copy(owner_hbm, owner_ref, ld_sem.at[4])
    ld_fill = pltpu.make_async_copy(fill_hbm, fill_ref, ld_sem.at[5])
    wcol = pl.multiple_of((b // (BLK // WIN)) * BLK, BLK)

    def win_copy():
        return pltpu.make_async_copy(table_hbm.at[:, pl.ds(wcol, BLK)], win_v, ld_sem.at[6])

    for load in (ld_ve, ld_ce, ld_val, ld_con):
        load.start()

    @pl.when(p == 0)
    def _():
        win_copy().start()

    ld_owner.start()
    ld_fill.start()
    ld_table = pltpu.make_async_copy(table_hbm, table_v, tb_sem)
    ld_table.start()

    lane = lax.broadcasted_iota(jnp.int32, (1, BLK), 1)
    mine_v = jnp.zeros((1, BLK), f32)
    mine_c = jnp.zeros((1, BLK), f32)
    ld_ve.wait()
    ld_ce.wait()
    for j in range(VAL):
        mine_v = jnp.where(lane % VAL == j, ve_ref[j], mine_v)
    for j in range(CON):
        mine_c = jnp.where(lane % CON == j, ce_ref[j], mine_c)
    energy[b] = jnp.concatenate([mine_v, mine_c], axis=0)
    ld_val.wait()
    ld_con.wait()
    val_f = val_v[...].astype(f32)
    con_g = con_v[...].astype(f32)
    val_f = jnp.concatenate([val_f[:, i : i + val_cols] for i in range(0, r, val_cols)], axis=0)
    con_g = jnp.concatenate([con_g[:, i : i + con_cols] for i in range(0, r, con_cols)], axis=0)

    def rows_of(group):
        return pl.ds(pl.multiple_of(group * GROUP, GROUP), GROUP)

    packed[rows_of(b), :] = jnp.concatenate([val_f, con_g], axis=1).astype(bf16)

    @pl.when(p == 0)
    def _():
        win_copy().wait()
        turned[...] = win_v[...].astype(f32).T
        first = pl.multiple_of(lax.rem(b, BLK // WIN) * WIN, WIN)
        bw[...] = turned[pl.ds(first, WIN), :].astype(bf16)

    pl.semaphore_wait(barrier, nb + ng - 2)

    def gather_copy(i, group):
        return pltpu.make_async_remote_copy(
            src_ref=packed.at[rows_of(group)],
            dst_ref=packed.at[rows_of(group)],
            send_sem=gs_sem,
            recv_sem=gr_sem.at[i],
            device_id={"band": lax.rem(b + 2 * i + core, nb)},
        )

    def forward_copy(group):
        return pltpu.make_async_remote_copy(
            src_ref=packed.at[rows_of(group)],
            dst_ref=packed.at[rows_of(group)],
            send_sem=fs_sem,
            recv_sem=fr_sem,
            device_id={"gblk": partner},
        )

    def many_copy(count, send_sem, recv_sem):
        rows = packed.at[pl.ds(0, count * GROUP)]
        return pltpu.make_async_remote_copy(
            src_ref=rows,
            dst_ref=rows,
            send_sem=send_sem,
            recv_sem=recv_sem,
            device_id={"gblk": partner},
        )

    def energy_copy(d):
        return pltpu.make_async_remote_copy(
            src_ref=energy.at[b],
            dst_ref=energy.at[b],
            send_sem=es_sem,
            recv_sem=er_sem,
            device_id={"band": lax.rem(b + d, nb)},
        )

    def energies_copy():
        return pltpu.make_async_remote_copy(
            src_ref=energy.at[pl.ds(0, nb - 1)],
            dst_ref=energy.at[pl.ds(0, nb - 1)],
            send_sem=es_sem,
            recv_sem=er_sem,
            device_id={"gblk": partner},
        )

    def window_copy(i, target):
        return pltpu.make_async_remote_copy(
            src_ref=bw,
            dst_ref=bw,
            send_sem=ws_sem.at[i],
            recv_sem=wr_sem,
            device_id={"gblk": target},
        )

    @pl.when(p == 0)
    def _():
        for i in range(ng // 2 - 1, 0, -1):
            window_copy(i, 2 * i).start()

    for i in steps:
        if i == 0:

            @pl.when(core == 1)
            def _():
                gather_copy(0, b).start()

        else:
            gather_copy(i, b).start()

    @pl.when(p == 0)
    def _():
        window_copy(0, partner).start()

    for d in border:
        energy_copy(d).start()

    def slots_of(o, carry):
        count = jnp.int32(0)
        first = jnp.int32(blocks)
        second = jnp.int32(blocks)
        third = jnp.int32(blocks)
        for j in range(blocks):
            hit = owner_ref[p * blocks + j] == o
            first = jnp.where(hit & (count == 0), j, first)
            second = jnp.where(hit & (count == 1), j, second)
            third = jnp.where(hit & (count == 2), j, third)
            count = count + jnp.where(hit, 1, 0)
        slot_s[o * CAP] = first
        slot_s[o * CAP + 1] = second
        slot_s[o * CAP + 2] = third
        return carry

    ld_owner.wait()
    ld_fill.wait()
    lax.fori_loop(0, ng, slots_of, 0)
    chi[blocks] = jnp.zeros((WIN, BLK), bf16)

    def pass_on(i):
        group = lax.rem(b + nb - 2 * i - core, nb)
        gather_copy(i, group).wait_recv()
        forward_copy(group).start()

    for i in reversed(steps):
        if i == 0:

            @pl.when(core == 1)
            def _():
                pass_on(0)

        else:
            pass_on(i)

    @pl.when(p > 0)
    def _():
        window_copy(0, partner).wait_recv()

    @pl.when((core == 0) & (p > 0))
    def _():
        window_copy(0, partner).start()

    energies_copy().wait_recv()

    on_lanes = jnp.zeros((1, vals), f32)
    con_lanes = jnp.zeros((1, vals), f32)
    for g in range(nb):
        on_lanes = jnp.where(lane // VAL == g, energy[g, 0:1, :], on_lanes)
        con_lanes = jnp.where(lane // CON == g, energy[g, 1:2, :], con_lanes)
    clane = lax.broadcasted_iota(jnp.int32, (cons, vals), 1)
    crow = lax.broadcasted_iota(jnp.int32, (cons, vals), 0)
    on_rows = jnp.sum(jnp.where(clane == crow, con_lanes, 0.0), axis=1, keepdims=True)
    weight = factor / (on_lanes - on_rows)
    wrow = lax.broadcasted_iota(jnp.int32, (WIN, 1), 0) + lax.rem(b, BLK // WIN) * WIN
    win_live = (wrow < fill_ref[b // (BLK // WIN)]).astype(f32)
    window = bw[...].astype(f32) * win_live

    @pl.when(core == 0)
    def _():
        many_copy(pairs, fs_sem, fr_sem).wait_recv()

    @pl.when(core == 1)
    def _():
        many_copy(pairs - 1, fs_sem, fr_sem).wait_recv()

    for g in range(0, nb, 2):
        one = packed[g * GROUP : (g + 1) * GROUP, :].astype(f32)
        two = packed[(g + 1) * GROUP : (g + 2) * GROUP, :].astype(f32)
        for i in range(r // val_cols):
            both = jnp.concatenate(
                [t[i * VAL : (i + 1) * VAL, 0:val_cols] for t in (one, two)], axis=0
            )
            val_m[g * VAL : (g + 2) * VAL, i * val_cols : (i + 1) * val_cols] = both.astype(bf16)
        for i in range(r // con_cols):
            both = jnp.concatenate(
                [t[i * CON : (i + 1) * CON, val_cols:] for t in (one, two)], axis=0
            )
            con_f[g * CON : (g + 2) * CON, i * con_cols : (i + 1) * con_cols] = both

    for h in range(WIN):
        x_s[h * cons : (h + 1) * cons, :] = (con_f[...] * window[h : h + 1, :]).astype(bf16)
    group_h = 4
    rows_h = group_h * cons
    weight_t = jnp.concatenate([weight] * group_h, axis=0)
    for q in range(WIN // group_h):
        chunk = slice(q * rows_h, (q + 1) * rows_h)
        raw = lax.dot_general(
            x_s[chunk, :], val_m[...], (((1,), (1,)), ((), ())), preferred_element_type=f32
        )
        s_s[chunk, :] = (raw * weight_t).astype(bf16)
    for q in range(WIN // group_h):
        chunk = slice(q * rows_h, (q + 1) * rows_h)
        full = jnp.dot(s_s[chunk, :], val_m[...], preferred_element_type=f32)
        for i in range(group_h):
            part = full[i * cons : (i + 1) * cons, :] * con_f[...]
            h = q * group_h + i
            m_s[h : h + 1, :] = jnp.sum(part, axis=0, keepdims=True)

    m_hi = m_s[...].astype(bf16)
    m_lo = (m_s[...] - m_hi.astype(f32)).astype(bf16)
    m_two = jnp.concatenate([m_hi, m_lo], axis=0)

    my_slots = pl.ds(pl.multiple_of(p * CAP * BLK, CAP * BLK), CAP * BLK)

    def owner_copy(o):
        return pltpu.make_async_remote_copy(
            src_ref=send.at[o],
            dst_ref=out_ref.at[:, my_slots],
            send_sem=cs_sem,
            recv_sem=cr_sem,
            device_id={"gblk": o},
        )

    ld_table.wait()
    step = 2
    for n in range(0, blocks, step):
        wide = jnp.dot(
            m_two, table_v[:, n * BLK : (n + step) * BLK], preferred_element_type=f32
        )
        wide = wide[0:WIN] + wide[WIN:]
        for j in range(step):
            rows = wide[:, j * BLK : (j + 1) * BLK]
            live = lane < fill_ref[p * blocks + n + j]
            chi[n + j] = jnp.where(live, rows, 0.0).astype(bf16)

    def fill_slots(o):
        for s in range(CAP):
            send[o, :, s * BLK : (s + 1) * BLK] = chi[slot_s[o * CAP + s]]

    for d in gorder:
        o = lax.rem(p + d, ng)
        fill_slots(o)
        owner_copy(o).start()
    fill_slots(p)
    own = pltpu.make_async_copy(send.at[p], out_ref.at[:, my_slots], own_sem)
    own.start()

    @pl.when(core == 0)
    def _():
        many_copy(pairs - 1, gs_sem, fr_sem).wait_send()
        many_copy(pairs - 1, fs_sem, fr_sem).wait_send()

    @pl.when(core == 1)
    def _():
        many_copy(pairs, gs_sem, fr_sem).wait_send()
        many_copy(pairs, fs_sem, fr_sem).wait_send()

    energies_copy().wait_send()

    @pl.when(p == 0)
    def _():
        for i in range(ng // 2):
            window_copy(i, partner).wait_send()

    @pl.when((core == 0) & (p > 0))
    def _():
        window_copy(0, partner).wait_send()

    own.wait()
    others = (ng - 1) * CAP * BLK
    all_copies = pltpu.make_async_remote_copy(
        src_ref=send.at[pl.ds(0, ng - 1)],
        dst_ref=out_ref.at[:, pl.ds(0, others)],
        send_sem=cs_sem,
        recv_sem=cr_sem,
        device_id={"gblk": partner},
    )
    all_copies.wait_send()
    all_copies.wait_recv()


def per_device(nb, ng, psi_val, psi_con, val_energy, con_energy, sphere_basis, block_owner, block_fill):
    r, cols = sphere_basis.shape
    blocks = cols // BLK
    factor = 1.0 / math.sqrt(psi_val.shape[0] * nb * psi_con.shape[0] * nb)
    hbm = pl.BlockSpec(memory_space=pltpu.HBM)
    args = (psi_val, psi_con, val_energy, con_energy, block_owner, block_fill, sphere_basis)
    args = [pltpu.with_memory_space_constraint(a, pltpu.HBM) for a in args]
    slot_cols = ng * CAP * BLK
    dma = pltpu.SemaphoreType.DMA
    got = pl.pallas_call(
        functools.partial(kernel, nb, ng, factor),
        out_shape=jax.ShapeDtypeStruct((WIN, slot_cols), bf16),
        in_specs=[hbm] * len(args),
        out_specs=pl.BlockSpec(memory_space=pl.ANY),
        scratch_shapes=[
            pltpu.SMEM(val_energy.shape, f32),
            pltpu.SMEM(con_energy.shape, f32),
            pltpu.SMEM(block_owner.shape, jnp.int32),
            pltpu.SMEM(block_fill.shape, jnp.int32),
            pltpu.VMEM((VAL, r), bf16),
            pltpu.VMEM((CON, r), bf16),
            pltpu.VMEM((r, cols), bf16),
            pltpu.VMEM((r, BLK), bf16),
            pltpu.VMEM((nb * GROUP, r * (VAL + CON) // GROUP), bf16),
            pltpu.VMEM((nb, 2, BLK), f32),
            pltpu.VMEM((BLK, r), f32),
            pltpu.VMEM((WIN, r), bf16),
            pltpu.VMEM((nb * VAL, r), bf16),
            pltpu.VMEM((nb * CON, r), f32),
            pltpu.VMEM((WIN * nb * CON, r), bf16),
            pltpu.VMEM((WIN * nb * CON, nb * VAL), bf16),
            pltpu.VMEM((WIN, r), f32),
            pltpu.VMEM((blocks + 1, WIN, BLK), bf16),
            pltpu.VMEM((ng, WIN, CAP * BLK), bf16),
            pltpu.SMEM((ng * CAP,), jnp.int32),
            dma((7,)),
            dma(()),
            dma(()),
            dma((nb // 2,)),
            dma(()),
            dma(()),
            dma(()),
            dma(()),
            dma((ng // 2,)),
            dma(()),
            dma(()),
            dma(()),
            dma(()),
        ],
        name="polarizability",
        compiler_params=pltpu.CompilerParams(
            collective_id=0, has_side_effects=True, vmem_limit_bytes=48 * 1024 * 1024
        ),
    )(*args)
    return got.astype(f32).T


def solution(mesh):
    nb, ng = mesh.shape["band"], mesh.shape["gblk"]
    return jax.shard_map(
        functools.partial(per_device, nb, ng),
        mesh=mesh,
        in_specs=(
            P("band", None),
            P("band", None),
            P("band"),
            P("band"),
            P(None, "gblk"),
            P(),
            P(),
        ),
        out_specs=P("gblk", "band"),
        check_vma=False,
    )
```

time: 32 us -> 27.9 us (0.87)
  Pallas kernels: 30.1 us -> 27 us
  other arithmetic: 1.7 us -> 0.77 us
    pallas_call x1, Pallas kernels: 30.1 us -> 27 us  [per_device(): pl.pallas_call(functools.partial(kernel, nb, ng, factor), out_shape=jax.S...]
    transpose x1, other arithmetic: 1.7 us -> 0.77 us  [per_device(): return got.astype(f32).T]
where the time goes in v3:
time: 27.9 us; the launch traced here: 27.8 us
  Pallas kernels  27 us (97%)
  other arithmetic  0.77 us (3%)
    pallas_call x1, Pallas kernels, per_device(): pl.pallas_call(functools.partial(kernel, nb, ng, factor), out_shape=jax.S...  27 us
    transpose x1, other arithmetic, per_device(): return got.astype(f32).T  0.77 us

profile of v3, /device:TPU:1, one launch (start us, length us, event | category | flops | bytes accessed | tf_op | source)
XLA Modules:
  0.0 27.8 jit_solution(14543403026095105154)
XLA Ops:
  0.0 27.0 %polarizability.1 = bf16[16,6144]{1,0:T(8,128)(2,1)S(1)} custom-call(bf16[8,1024]{1,0:T(8,128)(2,1)} %val_hbm.1, bf16[4,1024]{1,0:T(4,128)(2,1)} %con_hbm.1, f32[8]{0:T(128)} %ve_hbm.1, f32[4]{0:T(128)} %ce_hbm.1, s32[480]{0:T(512)} %owner_hbm.1, s32[480]{0:T(512)} %fill_hbm.1, bf16[1024,3840]{1,0:T(8,128)(2,1)} %table_hbm.1), custom_call_target="tpu_custom_call" | custom-call | tf_op jit(solution)/shard_map/polarizability/pallas_call | solution.py:414
  27.0 0.8 %convert_bitcast_fusion = f32[6144,16]{0,1:T(8,128)} fusion(bf16[16,6144]{1,0:T(8,128)(2,1)S(1)} %polarizability.1), kind=kLoop, calls=%fused_computation | loop fusion | flops 98304 | bytes 589824 | tf_op jit(solution)/shard_map/transpose | solution.py:459

commit v4 on v3

--- a/solution.py
+++ b/solution.py
@@ -17,20 +17,6 @@
 
 f32 = jnp.float32
 bf16 = jnp.bfloat16
-
-
-def far_first(n, hops):
-    return sorted(range(1, n), key=lambda d: -hops(d))
-
-
-def band_hops(d):
-    z = (d // 2) % 8
-    return min(z, 8 - z) + d % 2
-
-
-def gblk_hops(d):
-    x = d // 4
-    return min(x, 4 - x) + 2 * ((d // 2) % 2) + d % 2
 
 
 def kernel(
@@ -55,6 +41,7 @@
     win_v,
     packed,
     energy,
+    mine_e,
     turned,
     bw,
     val_m,
@@ -62,7 +49,6 @@
     x_s,
     s_s,
     m_s,
-    chi,
     send,
     slot_s,
     ld_sem,
@@ -86,17 +72,30 @@
     r = val_v.shape[1]
     vals, cons = nb * VAL, nb * CON
     val_cols, con_cols = r * VAL // GROUP, r * CON // GROUP
-    blocks = table_v.shape[1] // BLK
+    blocks = table_v.shape[0]
     pairs = nb // 2
-    border = far_first(nb, band_hops)
-    gorder = far_first(ng, gblk_hops)
+    z, y = b // 2, lax.rem(b, 2)
+    x, y_hi = p // 4, lax.rem(p // 2, 2)
+    turns = ng // 4
+
     steps = sorted(range(pairs), key=lambda i: -min(i, pairs - i))
+    moves = [(dx, dy, dc) for dx in range(turns) for dy in range(2) for dc in range(2)][1:]
+    moves.sort(key=lambda m: -(min(m[0], turns - m[0]) + 2 * m[1] + 0.1 * m[2]))
+
+    def band_at(i, flip):
+        return 2 * lax.rem(z + i, pairs) + lax.rem(y + flip, 2)
+
+    def gblk_at(move):
+        dx, dy, dc = move
+        return 4 * lax.rem(x + dx, turns) + 2 * lax.rem(y_hi + dy, 2) + lax.rem(core + dc, 2)
 
     barrier = pltpu.get_barrier_semaphore()
-    for d in border:
-        pl.semaphore_signal(barrier, 1, device_id={"band": lax.rem(b + d, nb)})
-    for d in gorder:
-        pl.semaphore_signal(barrier, 1, device_id={"gblk": lax.rem(p + d, ng)})
+    for i in steps:
+        for flip in (1, 0):
+            if i or flip:
+                pl.semaphore_signal(barrier, 1, device_id={"band": band_at(i, flip)})
+    for move in moves:
+        pl.semaphore_signal(barrier, 1, device_id={"gblk": gblk_at(move)})
 
     ld_val = pltpu.make_async_copy(val_hbm, val_v, ld_sem.at[0])
     ld_con = pltpu.make_async_copy(con_hbm, con_v, ld_sem.at[1])
@@ -118,8 +117,10 @@
 
     ld_owner.start()
     ld_fill.start()
-    ld_table = pltpu.make_async_copy(table_hbm, table_v, tb_sem)
-    ld_table.start()
+    for j in range(blocks):
+        pltpu.make_async_copy(
+            table_hbm.at[:, j * BLK : (j + 1) * BLK], table_v.at[j], tb_sem
+        ).start()
 
     lane = lax.broadcasted_iota(jnp.int32, (1, BLK), 1)
     mine_v = jnp.zeros((1, BLK), f32)
@@ -130,7 +131,12 @@
         mine_v = jnp.where(lane % VAL == j, ve_ref[j], mine_v)
     for j in range(CON):
         mine_c = jnp.where(lane % CON == j, ce_ref[j], mine_c)
-    energy[b] = jnp.concatenate([mine_v, mine_c], axis=0)
+    mine_e[...] = jnp.concatenate([mine_v, mine_c], axis=0)
+
+    @pl.when(core == 0)
+    def _():
+        energy[y, z] = mine_e[...]
+
     ld_val.wait()
     ld_con.wait()
     val_f = val_v[...].astype(f32)
@@ -158,7 +164,7 @@
             dst_ref=packed.at[rows_of(group)],
             send_sem=gs_sem,
             recv_sem=gr_sem.at[i],
-            device_id={"band": lax.rem(b + 2 * i + core, nb)},
+            device_id={"band": band_at(i, core)},
         )
 
     def forward_copy(group):
@@ -180,21 +186,22 @@
             device_id={"gblk": partner},
         )
 
-    def energy_copy(d):
-        return pltpu.make_async_remote_copy(
-            src_ref=energy.at[b],
-            dst_ref=energy.at[b],
-            send_sem=es_sem,
-            recv_sem=er_sem,
-            device_id={"band": lax.rem(b + d, nb)},
-        )
-
-    def energies_copy():
-        return pltpu.make_async_remote_copy(
-            src_ref=energy.at[pl.ds(0, nb - 1)],
-            dst_ref=energy.at[pl.ds(0, nb - 1)],
-            send_sem=es_sem,
-            recv_sem=er_sem,
+    def energy_copy(i):
+        return pltpu.make_async_remote_copy(
+            src_ref=mine_e,
+            dst_ref=energy.at[y, z],
+            send_sem=es_sem.at[0],
+            recv_sem=er_sem.at[0],
+            device_id={"band": band_at(i, core)},
+        )
+
+    def energies_copy(count, k):
+        rows = energy.at[lax.rem(y + core, 2), pl.ds(0, count)]
+        return pltpu.make_async_remote_copy(
+            src_ref=rows,
+            dst_ref=rows,
+            send_sem=es_sem.at[k],
+            recv_sem=er_sem.at[k],
             device_id={"gblk": partner},
         )
 
@@ -212,22 +219,22 @@
         for i in range(ng // 2 - 1, 0, -1):
             window_copy(i, 2 * i).start()
 
-    for i in steps:
-        if i == 0:
-
-            @pl.when(core == 1)
-            def _():
-                gather_copy(0, b).start()
-
-        else:
-            gather_copy(i, b).start()
+    early = 3
+    for i in steps[:early]:
+        gather_copy(i, b).start()
+    for i in steps[:-1]:
+        energy_copy(i).start()
+    for i in steps[early:-1]:
+        gather_copy(i, b).start()
+
+    @pl.when(core == 1)
+    def _():
+        energy_copy(0).start()
+        gather_copy(0, b).start()
 
     @pl.when(p == 0)
     def _():
         window_copy(0, partner).start()
-
-    for d in border:
-        energy_copy(d).start()
 
     def slots_of(o, carry):
         count = jnp.int32(0)
@@ -248,22 +255,30 @@
     ld_owner.wait()
     ld_fill.wait()
     lax.fori_loop(0, ng, slots_of, 0)
-    chi[blocks] = jnp.zeros((WIN, BLK), bf16)
 
     def pass_on(i):
-        group = lax.rem(b + nb - 2 * i - core, nb)
+        group = band_at(pairs - i, core)
         gather_copy(i, group).wait_recv()
         forward_copy(group).start()
 
-    for i in reversed(steps):
-        if i == 0:
-
-            @pl.when(core == 1)
-            def _():
-                pass_on(0)
-
-        else:
-            pass_on(i)
+    @pl.when(core == 1)
+    def _():
+        pass_on(0)
+
+    for i in steps[-2:2:-1]:
+        pass_on(i)
+
+    @pl.when(core == 0)
+    def _():
+        energies_copy(pairs - 1, 0).wait_recv()
+
+    @pl.when(core == 1)
+    def _():
+        energies_copy(pairs, 0).wait_recv()
+
+    energies_copy(pairs, 1).start()
+    for i in steps[2::-1]:
+        pass_on(i)
 
     @pl.when(p > 0)
     def _():
@@ -273,13 +288,14 @@
     def _():
         window_copy(0, partner).start()
 
-    energies_copy().wait_recv()
+    energies_copy(pairs, 1).wait_recv()
 
     on_lanes = jnp.zeros((1, vals), f32)
     con_lanes = jnp.zeros((1, vals), f32)
     for g in range(nb):
-        on_lanes = jnp.where(lane // VAL == g, energy[g, 0:1, :], on_lanes)
-        con_lanes = jnp.where(lane // CON == g, energy[g, 1:2, :], con_lanes)
+        both = energy[g % 2, g // 2]
+        on_lanes = jnp.where(lane // VAL == g, both[0:1], on_lanes)
+        con_lanes = jnp.where(lane // CON == g, both[1:2], con_lanes)
     clane = lax.broadcasted_iota(jnp.int32, (cons, vals), 1)
     crow = lax.broadcasted_iota(jnp.int32, (cons, vals), 0)
     on_rows = jnp.sum(jnp.where(clane == crow, con_lanes, 0.0), axis=1, keepdims=True)
@@ -344,41 +360,56 @@
             device_id={"gblk": o},
         )
 
-    ld_table.wait()
-    step = 2
-    for n in range(0, blocks, step):
-        wide = jnp.dot(
-            m_two, table_v[:, n * BLK : (n + step) * BLK], preferred_element_type=f32
-        )
+    lanes = lax.broadcasted_iota(jnp.int32, (1, CAP * BLK), 1)
+
+    def fill_slots(owners):
+        table = []
+        limits = []
+        for o in owners:
+            limit = jnp.zeros((1, CAP * BLK), jnp.int32)
+            for s in range(CAP):
+                block = slot_s[o * CAP + s]
+                j = jnp.minimum(block, blocks - 1)
+                live = jnp.where(block < blocks, fill_ref[p * blocks + j], 0)
+                limit = jnp.where(lanes // BLK == s, live, limit)
+                table.append(table_v[j])
+            limits.append(limit)
+        wide = jnp.dot(m_two, jnp.concatenate(table, axis=1), preferred_element_type=f32)
         wide = wide[0:WIN] + wide[WIN:]
-        for j in range(step):
-            rows = wide[:, j * BLK : (j + 1) * BLK]
-            live = lane < fill_ref[p * blocks + n + j]
-            chi[n + j] = jnp.where(live, rows, 0.0).astype(bf16)
-
-    def fill_slots(o):
-        for s in range(CAP):
-            send[o, :, s * BLK : (s + 1) * BLK] = chi[slot_s[o * CAP + s]]
-
-    for d in gorder:
-        o = lax.rem(p + d, ng)
-        fill_slots(o)
-        owner_copy(o).start()
-    fill_slots(p)
+        for i, o in enumerate(owners):
+            rows = wide[:, i * CAP * BLK : (i + 1) * CAP * BLK]
+            send[o] = jnp.where(lanes % BLK < limits[i], rows, 0.0).astype(bf16)
+
+    pltpu.make_async_copy(table_v, table_v, tb_sem).wait()
+
+    done = 0
+    for size in (4, 5, 6):
+        owners = [gblk_at(move) for move in moves[done : done + size]]
+        done += size
+        fill_slots(owners)
+
+        @pl.when(p < ng)
+        def _(owners=owners):
+            for o in owners:
+                owner_copy(o).start()
+
+    fill_slots([p])
     own = pltpu.make_async_copy(send.at[p], out_ref.at[:, my_slots], own_sem)
     own.start()
 
     @pl.when(core == 0)
     def _():
+        energies_copy(pairs - 1, 0).wait_send()
         many_copy(pairs - 1, gs_sem, fr_sem).wait_send()
         many_copy(pairs - 1, fs_sem, fr_sem).wait_send()
 
     @pl.when(core == 1)
     def _():
+        energies_copy(pairs, 0).wait_send()
         many_copy(pairs, gs_sem, fr_sem).wait_send()
         many_copy(pairs, fs_sem, fr_sem).wait_send()
 
-    energies_copy().wait_send()
+    energies_copy(pairs, 1).wait_send()
 
     @pl.when(p == 0)
     def _():
@@ -423,10 +454,11 @@
             pltpu.SMEM(block_fill.shape, jnp.int32),
             pltpu.VMEM((VAL, r), bf16),
             pltpu.VMEM((CON, r), bf16),
-            pltpu.VMEM((r, cols), bf16),
+            pltpu.VMEM((blocks, r, BLK), bf16),
             pltpu.VMEM((r, BLK), bf16),
             pltpu.VMEM((nb * GROUP, r * (VAL + CON) // GROUP), bf16),
-            pltpu.VMEM((nb, 2, BLK), f32),
+            pltpu.VMEM((2, nb // 2, 2, BLK), f32),
+            pltpu.VMEM((2, BLK), f32),
             pltpu.VMEM((BLK, r), f32),
             pltpu.VMEM((WIN, r), bf16),
             pltpu.VMEM((nb * VAL, r), bf16),
@@ -434,7 +466,6 @@
             pltpu.VMEM((WIN * nb * CON, r), bf16),
             pltpu.VMEM((WIN * nb * CON, nb * VAL), bf16),
             pltpu.VMEM((WIN, r), f32),
-            pltpu.VMEM((blocks + 1, WIN, BLK), bf16),
             pltpu.VMEM((ng, WIN, CAP * BLK), bf16),
             pltpu.SMEM((ng * CAP,), jnp.int32),
             dma((7,)),
@@ -443,8 +474,8 @@
             dma((nb // 2,)),
             dma(()),
             dma(()),
-            dma(()),
-            dma(()),
+            dma((2,)),
+            dma((2,)),
             dma((ng // 2,)),
             dma(()),
             dma(()),

time: 27.9 us -> 26.7 us (0.957)
  Pallas kernels: 27 us -> 25.8 us
    pallas_call x1, Pallas kernels: 27 us -> 25.8 us  [per_device(): pl.pallas_call(functools.partial(kernel, nb, ng, factor), out_shape=jax.S...]
where the time goes in v4:
time: 26.7 us; the launch traced here: 26.6 us
  Pallas kernels  25.8 us (97%)
  other arithmetic  0.77 us (3%)
    pallas_call x1, Pallas kernels, per_device(): pl.pallas_call(functools.partial(kernel, nb, ng, factor), out_shape=jax.S...  25.8 us
    transpose x1, other arithmetic, per_device(): return got.astype(f32).T  0.77 us

profile of v4, /device:TPU:1, one launch (start us, length us, event | category | flops | bytes accessed | tf_op | source)
XLA Modules:
  0.0 26.6 jit_solution(1063746506868210113)
XLA Ops:
  0.0 25.8 %polarizability.1 = bf16[16,6144]{1,0:T(8,128)(2,1)S(1)} custom-call(bf16[8,1024]{1,0:T(8,128)(2,1)} %val_hbm.1, bf16[4,1024]{1,0:T(4,128)(2,1)} %con_hbm.1, f32[8]{0:T(128)} %ve_hbm.1, f32[4]{0:T(128)} %ce_hbm.1, s32[480]{0:T(512)} %owner_hbm.1, s32[480]{0:T(512)} %fill_hbm.1, bf16[1024,3840]{1,0:T(8,128)(2,1)} %table_hbm.1), custom_call_target="tpu_custom_call" | custom-call | tf_op jit(solution)/shard_map/polarizability/pallas_call | solution.py:445
  25.9 0.8 %convert_bitcast_fusion = f32[6144,16]{0,1:T(8,128)} fusion(bf16[16,6144]{1,0:T(8,128)(2,1)S(1)} %polarizability.1), kind=kLoop, calls=%fused_computation | loop fusion | flops 98304 | bytes 589824 | tf_op jit(solution)/shard_map/transpose | solution.py:490

commit v5 on v4

--- a/solution.py
+++ b/solution.py
@@ -261,24 +261,24 @@
         gather_copy(i, group).wait_recv()
         forward_copy(group).start()
 
+    for i in steps[:4]:
+        pass_on(i)
+
+    @pl.when(core == 0)
+    def _():
+        energies_copy(pairs - 1, 0).wait_recv()
+
     @pl.when(core == 1)
     def _():
+        energies_copy(pairs, 0).wait_recv()
+
+    energies_copy(pairs, 1).start()
+    for i in steps[4:-1]:
+        pass_on(i)
+
+    @pl.when(core == 1)
+    def _():
         pass_on(0)
-
-    for i in steps[-2:2:-1]:
-        pass_on(i)
-
-    @pl.when(core == 0)
-    def _():
-        energies_copy(pairs - 1, 0).wait_recv()
-
-    @pl.when(core == 1)
-    def _():
-        energies_copy(pairs, 0).wait_recv()
-
-    energies_copy(pairs, 1).start()
-    for i in steps[2::-1]:
-        pass_on(i)
 
     @pl.when(p > 0)
     def _():

time: 26.7 us -> 26.7 us (level)
  no operation moved by 1% of the time
where the time goes in v5:
time: 26.7 us; the launch traced here: 26.6 us
  Pallas kernels  25.8 us (97%)
  other arithmetic  0.77 us (3%)
    pallas_call x1, Pallas kernels, per_device(): pl.pallas_call(functools.partial(kernel, nb, ng, factor), out_shape=jax.S...  25.8 us
    transpose x1, other arithmetic, per_device(): return got.astype(f32).T  0.77 us

profile of v5, /device:TPU:1, one launch (start us, length us, event | category | flops | bytes accessed | tf_op | source)
XLA Modules:
  0.0 26.6 jit_solution(9976868517446090058)
XLA Ops:
  0.0 25.8 %polarizability.1 = bf16[16,6144]{1,0:T(8,128)(2,1)S(1)} custom-call(bf16[8,1024]{1,0:T(8,128)(2,1)} %val_hbm.1, bf16[4,1024]{1,0:T(4,128)(2,1)} %con_hbm.1, f32[8]{0:T(128)} %ve_hbm.1, f32[4]{0:T(128)} %ce_hbm.1, s32[480]{0:T(512)} %owner_hbm.1, s32[480]{0:T(512)} %fill_hbm.1, bf16[1024,3840]{1,0:T(8,128)(2,1)} %table_hbm.1), custom_call_target="tpu_custom_call" | custom-call | tf_op jit(solution)/shard_map/polarizability/pallas_call | solution.py:445
  25.8 0.8 %convert_bitcast_fusion = f32[6144,16]{0,1:T(8,128)} fusion(bf16[16,6144]{1,0:T(8,128)(2,1)S(1)} %polarizability.1), kind=kLoop, calls=%fused_computation | loop fusion | flops 98304 | bytes 589824 | tf_op jit(solution)/shard_map/transpose | solution.py:490
